TPU v7x, 32 devices: a whole 2x2x4 slice. The times are simulated.
32 devices in a mesh: groups: 2 (over y), seq: 4 (over z), mp: 2 (over x), rep: 2 (over core).
Axes of the slice: x: 2, y: 2, z: 4, core: 2. Of those that a mesh axis runs over, the one named last changes fastest.
Arguments:
- query_states: bfloat16 [8, 512, 2048], P(('groups', 'mp', 'rep'), 'seq'), parts along dimension 0, may hold values from -10 to 10
- key_states: bfloat16 [8, 512, 2048], P(('groups', 'mp', 'rep'), 'seq'), parts along dimension 0, may hold values from -10 to 10
- value_states: bfloat16 [8, 512, 2048], P(('groups', 'mp', 'rep'), 'seq'), parts along dimension 0, may hold values from -6 to 6
- out_grad: bfloat16 [8, 512, 2048], P(('groups', 'mp', 'rep'), 'seq'), parts along dimension 0, may hold values from -12 to 12
- pattern: int32 [16, 4, 6], P('seq'), may hold values from 0 to 3, as said below
- counts: int32 [16, 4], P('seq'), may hold values from 1 to 6, as said below
Outputs:
- query_grad: bfloat16 [8, 512, 2048], P(('groups', 'mp', 'rep'), 'seq'), parts along dimension 0
- key_grad: bfloat16 [8, 512, 2048], P(('groups', 'mp', 'rep'), 'seq'), parts along dimension 0
- value_grad: bfloat16 [8, 512, 2048], P(('groups', 'mp', 'rep'), 'seq'), parts along dimension 0
There are 2 independent parts, one for each index of `groups`. A program takes and returns all parts, laid end to end along the dimension named above; an argument that names none is the same for every part. Nothing has to cross between parts.
Inputs may be any that keep to these rules, and one draw needn't show every extreme that they name: pattern[h, i, 0] = i; only the first counts[h, i] entries of a row are used, and a row may name a block more than once. `counts`: the number of used entries of each row of pattern.
All inputs are finite; a program needn't handle non-finite values.
Results may differ from a plain program's by a relative error of at most 0.012.
Values may be sent and summed in bfloat16 or wider, within the bound.
No kernel may reach another device: no remote copies, remote signals or barrier semaphores. Data moves between devices by JAX's collectives and lax.ppermute only.
A program may use at most 64 MiB of HBM per device.

v0:
```python
import functools
import math

import jax
import jax.numpy as jnp
from jax import lax
from jax.experimental import pallas as pl
from jax.experimental.pallas import tpu as pltpu
from jax.sharding import PartitionSpec as P

LOG2E = math.log2(math.e)
NT = (((1,), (1,)), ((), ()))
NN = (((1,), (0,)), ((), ()))
TN = (((0,), (0,)), ((), ()))
VMEM_LIMIT = 32 * 1024 * 1024
SMEM = pl.BlockSpec(memory_space=pltpu.SMEM)
ANY = pl.BlockSpec(memory_space=pl.ANY)
VMEM = pl.BlockSpec(memory_space=pltpu.VMEM)
PARAMS = pltpu.CompilerParams(vmem_limit_bytes=VMEM_LIMIT)
LITTLE = pltpu.CompilerParams(vmem_limit_bytes=4 * 1024 * 1024)
SIZES = ((3, 2), (3, 3), (4, 3), (4, 4), (5, 5))


def dot(left, right, dims=NN):
    return lax.dot_general(left, right, dims, preferred_element_type=jnp.float32)


def shift(array, step):
    size = lax.axis_size("seq")
    return lax.ppermute(array, "seq", [(j, (j + step) % size) for j in range(size)])


def table_kernel(heads, blocks, slots, pattern, counts, table):
    def one_row(index, carry):
        head, row = index // blocks, index % blocks
        count = counts[head, row]
        named = [jnp.where(slot < count, pattern[head, row, slot], blocks) for slot in range(slots)]
        for column in range(blocks):
            table[head, row * blocks + column] = sum((n == column).astype(jnp.int32) for n in named)
        return carry

    if heads * blocks > 16:
        lax.fori_loop(0, heads * blocks, one_row, 0)
    else:
        for index in range(heads * blocks):
            one_row(index, 0)


def count_uses(pattern, counts):
    heads, blocks, slots = pattern.shape
    return pl.pallas_call(
        functools.partial(table_kernel, heads, blocks, slots),
        out_shape=jax.ShapeDtypeStruct((heads, blocks * blocks), jnp.int32),
        in_specs=[SMEM] * 2,
        out_specs=SMEM,
        name="count_uses",
    )(pattern, counts)


class Rows:
    def __init__(self, total):
        self.slots = total
        self.lists = 2 * total
        self.tallies = self.lists + max(max(pair) for pair in SIZES)
        self.shared = self.tallies + 1
        self.spot = self.shared + 1
        self.count = -(-(self.spot + 1) // 8) * 8


def plan_kernel(size, heads, place, *refs):
    parts, (plan, choice, held) = refs[:size], refs[size:]
    position = place[0]
    total, pairs = size * heads, size * size
    rows = Rows(total)
    count = parts[0].shape[-1]
    for step in range(size):
        for row in range(size):
            named = parts[step][:, row, :].astype(jnp.float32)
            held[pl.ds(step * heads, heads), pl.ds(row * count, count)] = named
    head = lax.broadcasted_iota(jnp.int32, (total, total), 0)
    place_of = lax.broadcasted_iota(jnp.int32, (total, total), 1)
    step = sum((place_of >= heads * k).astype(jnp.int32) for k in range(1, size))
    owner = position - step
    owner += jnp.where(owner < 0, size, 0)
    order = (head == owner * heads + place_of - step * heads).astype(jnp.float32)
    named = dot(order, held[...])
    head = lax.broadcasted_iota(jnp.int32, (total, pairs), 0)
    pair = lax.broadcasted_iota(jnp.int32, (total, pairs), 1)
    table = jnp.zeros((total, pairs), jnp.float32)
    for row in range(size):
        column = (pair - row * size).astype(jnp.float32)
        for slot in range(row * count, (row + 1) * count):
            table += jnp.where(column == named[:, slot : slot + 1], 1.0, 0.0)
    plan[pl.ds(0, total), :] = table.astype(jnp.int32)

    uses = (table > 0).astype(jnp.float32)
    for block in range(size):
        uses = jnp.where(pair == block * (size + 1), 0.0, uses)
    lane = lax.broadcasted_iota(jnp.int32, (1, pairs), 1)
    shared, mine = jnp.zeros((1, pairs), jnp.int32), jnp.zeros((1, 1), jnp.int32)
    number = head[:, :1].astype(jnp.float32)
    free = number >= 0
    for index in range(size):
        load = jnp.sum(uses, axis=0, keepdims=True)
        score = jnp.sum(uses * (load * load * load), axis=1, keepdims=True)
        score = jnp.where(free, score * total + number, -1.0)
        top = jnp.max(score, axis=0, keepdims=True)
        uses = jnp.where(score == top, 0.0, uses)
        free = free & (score != top)
        name = (top - total * jnp.floor(top * (1.0 / total))).astype(jnp.int32)
        shared = jnp.where(lane == index, name, shared)
        mine = jnp.where(index == position, name, mine)
    earlier = lax.broadcasted_iota(jnp.int32, (total, total), 1) < lax.broadcasted_iota(jnp.int32, (total, total), 0)
    slots = dot(earlier.astype(jnp.float32), uses)
    tallies = jnp.sum(uses, axis=0, keepdims=True)
    plan[pl.ds(rows.slots, total), :] = slots.astype(jnp.int32)
    for slot in range(rows.tallies - rows.lists):
        hit = jnp.where(slots == slot, uses * head.astype(jnp.float32), 0.0)
        plan[pl.ds(rows.lists + slot, 1), :] = jnp.sum(hit, axis=0, keepdims=True).astype(jnp.int32)
    plan[pl.ds(rows.tallies, 1), :] = tallies.astype(jnp.int32)
    plan[pl.ds(rows.shared, 1), :] = shared
    plan[pl.ds(rows.spot, 1), :] = jnp.where(lane == 0, position, mine)

    odd = functools.reduce(
        jnp.logical_or, [lane == i * size + j for i in range(size) for j in range(size) if (i - j) % 2]
    )
    most_odd = jnp.max(jnp.where(odd, tallies, 0.0)).astype(jnp.int32)
    most_even = jnp.max(jnp.where(odd, 0.0, tallies)).astype(jnp.int32)
    chosen = jnp.int32(len(SIZES))
    for index in reversed(range(len(SIZES))):
        fits = (most_odd <= SIZES[index][0]) & (most_even <= SIZES[index][1])
        chosen = jnp.where(fits, index, chosen)
    choice[0] = chosen


def make_plan(size, heads, place, parts):
    total, pairs = size * heads, size * size
    return pl.pallas_call(
        functools.partial(plan_kernel, size, heads),
        out_shape=[
            jax.ShapeDtypeStruct((Rows(total).count, pairs), jnp.int32),
            jax.ShapeDtypeStruct((1,), jnp.int32),
        ],
        in_specs=[SMEM] + [VMEM] * size,
        out_specs=[VMEM, SMEM],
        scratch_shapes=[pltpu.VMEM((total, size * parts[0].shape[2]), jnp.float32)],
        compiler_params=LITTLE,
        name="make_plan",
    )(place, *parts)


def pack_kernel(size, width, row, place, starts, *refs):
    sources, outs, (held, in_sems, out_sems) = refs[:4], refs[-2 - size : -3], refs[-3:]
    position = place[0]
    reads, writes = [], []
    for step in range(1, size):
        start = starts[row, lax.rem(position + step, size)] * width
        columns = pl.ds(pl.multiple_of(start, 128), width)
        reads.append(
            [
                pltpu.make_async_copy(
                    source.at[0, :, columns], held.at[step - 1, index], in_sems.at[step - 1, index]
                )
                for index, source in enumerate(sources)
            ]
        )
        writes.append(pltpu.make_async_copy(held.at[step - 1], outs[step - 1], out_sems.at[step - 1]))
    for read in sum(reads, []):
        read.start()
    for read, write in zip(reads, writes):
        for one in read:
            one.wait()
        write.start()
    for write in writes:
        write.wait()


def pack(size, width, row, place, starts, sources, after):
    tokens = sources[0].shape[1]
    return pl.pallas_call(
        functools.partial(pack_kernel, size, width, row),
        out_shape=[jax.ShapeDtypeStruct((4, tokens, width), jnp.bfloat16)] * (size - 1),
        in_specs=[SMEM] * 2 + [ANY] * (4 + len(after)),
        out_specs=[ANY] * (size - 1),
        scratch_shapes=[
            pltpu.VMEM((size - 1, 4, tokens, width), jnp.bfloat16),
            pltpu.SemaphoreType.DMA((size - 1, 4)),
            pltpu.SemaphoreType.DMA((size - 1,)),
        ],
        compiler_params=PARAMS,
        name="pack",
    )(place, starts, *sources, *after)


def heads_kernel(size, heads, block, spot, uses, *refs):
    own_refs, far_refs = refs[:4], refs[4 : 3 + size]
    out_refs = refs[-4 - size : -4]
    joined, key_flip, key_sum, value_sum = refs[-4:]
    position, first = spot[0], spot[2]
    tokens, features = own_refs[0].shape[1], joined.shape[2]
    length = size * tokens
    blocks = length // block
    local = tokens // block
    chunk = min(length, max(2 * block, 256))
    factor = features**-0.5

    def origin(index):
        return lax.rem(position + size - index // local, size) * local + index % local

    def one_chunk(head, number):
        start = pl.multiple_of(number * chunk, chunk)
        rows = pl.ds(start, chunk)
        query, grad = joined[0, rows, :], joined[3, rows, :]
        scores = dot(joined[1], query, NT)
        prob_grad = dot(joined[2], grad, NT)
        weight_parts, score_parts = [], []
        for part in range(chunk // block):
            row = origin(number * (chunk // block) + part)
            columns = slice(part * block, (part + 1) * block)
            counts = [
                uses[first + head, row * blocks + origin(j)].astype(jnp.float32) for j in range(blocks)
            ]
            terms = []
            for j in range(blocks):
                term = scores[j * block : (j + 1) * block, columns] * (factor * LOG2E)
                terms.append(term + jnp.where(counts[j] > 0, 0.0, -jnp.inf))
            top = functools.reduce(jnp.maximum, terms)
            top = jnp.max(top, axis=0, keepdims=True)
            exps = [jnp.exp2(term - top) for term in terms]
            grads = [prob_grad[j * block : (j + 1) * block, columns] for j in range(blocks)]
            total = sum(count * e for count, e in zip(counts, exps))
            moment = sum(count * (e * g) for count, e, g in zip(counts, exps, grads))
            inverse = 1.0 / jnp.sum(total, axis=0, keepdims=True)
            delta = jnp.sum(moment, axis=0, keepdims=True) * inverse
            probs = [e * (inverse * count) for count, e in zip(counts, exps)]
            weight_parts.append(jnp.concatenate([p.astype(jnp.bfloat16) for p in probs], axis=0))
            score_parts.append(
                jnp.concatenate(
                    [(p * (g - delta)).astype(jnp.bfloat16) for p, g in zip(probs, grads)], axis=0
                )
            )
        weights = jnp.concatenate(weight_parts, axis=1)
        score_grad = jnp.concatenate(score_parts, axis=1)
        key_sum[...] += dot(score_grad, query)
        value_sum[...] += dot(weights, grad)
        flipped = dot(key_flip[...], score_grad)
        return (flipped.T * factor).astype(jnp.bfloat16)

    def one_head(head, carry):
        features_at = columns_of(head, features)
        for index in range(4):
            joined[index, pl.ds(0, tokens), :] = own_refs[index][0, :, features_at]
            for step in range(1, size):
                joined[index, pl.ds(step * tokens, tokens), :] = far_refs[step - 1][index, :, features_at]
        key_flip[...] = joined[1].T
        key_sum[...] = jnp.zeros_like(key_sum)
        value_sum[...] = jnp.zeros_like(value_sum)

        for number in range(length // chunk):
            query_grad = one_chunk(head, number)
            for part in range(max(1, chunk // tokens)):
                step, within = divmod(number * chunk + part * tokens, tokens)
                span = min(chunk, tokens)
                out_refs[step][0, pl.ds(within, span), features_at] = query_grad[part * span : (part + 1) * span]
        for step in range(size):
            rows = pl.ds(step * tokens, tokens)
            out_refs[step][1, :, features_at] = (factor * key_sum[rows, :]).astype(jnp.bfloat16)
            out_refs[step][2, :, features_at] = value_sum[rows, :].astype(jnp.bfloat16)
        return carry

    if heads == 1:
        one_head(0, 0)
    else:
        lax.fori_loop(0, heads, one_head, 0)


def run_heads(size, heads, block, spot, uses, owns, fars, after=()):
    tokens = owns[0].shape[1]
    features = fars[0].shape[2] // heads
    width = heads * features
    length = size * tokens
    own_spec = pl.BlockSpec((1, tokens, width), lambda i, spot: (0, 0, spot[1]))
    far_spec = pl.BlockSpec((4, tokens, width), lambda i, spot: (0, 0, 0))
    out_spec = pl.BlockSpec((3, tokens, width), lambda i, spot: (0, 0, 0))
    return pl.pallas_call(
        functools.partial(heads_kernel, size, heads, block),
        grid_spec=pltpu.PrefetchScalarGridSpec(
            num_scalar_prefetch=1,
            grid=(1,),
            in_specs=[SMEM] + [own_spec] * 4 + [far_spec] * (size - 1) + [ANY] * len(after),
            out_specs=[out_spec] * size,
            scratch_shapes=[
                pltpu.VMEM((4, length, features), jnp.bfloat16),
                pltpu.VMEM((features, length), jnp.bfloat16),
                pltpu.VMEM((length, features), jnp.float32),
                pltpu.VMEM((length, features), jnp.float32),
            ],
        ),
        out_shape=[jax.ShapeDtypeStruct((3, tokens, width), jnp.bfloat16)] * size,
        compiler_params=PARAMS,
        cost_estimate=pl.CostEstimate(
            flops=heads * 10 * length * length * features,
            bytes_accessed=heads * 14 * length * features,
            transcendentals=heads * length * length,
        ),
        name="heads",
    )(spot, uses, *owns, *fars, *after)


def place_kernel(size, groups, width, place, *refs):
    parts, outs = refs[: size * groups], refs[size * groups : -3]
    held, in_sems, out_sems = refs[-3:]
    position = place[0]
    total = outs[0].shape[2]
    reads, writes = [], []
    for step in range(size):
        start = pl.multiple_of(lax.rem(position + step, size) * (total // size), 128)
        reads.append(
            [
                pltpu.make_async_copy(
                    parts[group * size + step],
                    held.at[step, :, :, pl.ds(group * width, width)],
                    in_sems.at[step, group],
                )
                for group in range(groups)
            ]
        )
        writes.append(
            [
                pltpu.make_async_copy(
                    held.at[step, index],
                    out.at[0, :, pl.ds(start, total // size)],
                    out_sems.at[step, index],
                )
                for index, out in enumerate(outs)
            ]
        )
    for read in sum(reads, []):
        read.start()
    for read, write in zip(reads, writes):
        for one in read:
            one.wait()
        for one in write:
            one.start()
    for one in sum(writes, []):
        one.wait()


def put_in_place(size, groups, width, place, parts, shape):
    return pl.pallas_call(
        functools.partial(place_kernel, size, groups, width),
        out_shape=[jax.ShapeDtypeStruct(shape, jnp.bfloat16)] * 3,
        in_specs=[SMEM] + [ANY] * len(parts),
        out_specs=[ANY] * 3,
        scratch_shapes=[
            pltpu.VMEM((size, 3, shape[1], groups * width), jnp.bfloat16),
            pltpu.SemaphoreType.DMA((size, groups)),
            pltpu.SemaphoreType.DMA((size, 3)),
        ],
        compiler_params=PARAMS,
        name="put_in_place",
    )(place, *parts)


def send_group(size, width, row, place, starts, sources, after=()):
    packed = pack(size, width, row, place, starts, sources, after)
    return [shift(packed[step - 1], step) for step in range(1, size)]


def dense_plan(size, heads, groups, block, place, uses, sources):
    features = sources[0].shape[2] // (uses.shape[0] * size)
    width = heads * features
    parts = []
    for group in range(groups):
        starts = jnp.arange(size, dtype=jnp.int32)[None] * groups + group
        spot = jnp.concatenate([place, place * groups + group, jnp.full(1, group * heads, jnp.int32)])
        fars = send_group(size, width, 0, place, starts, sources)
        outs = run_heads(size, heads, block, spot, uses, sources, fars)
        parts.append(outs[0])
        parts += [shift(outs[step], -step) for step in range(1, size)]
    return tuple(put_in_place(size, groups, width, place, parts, sources[0].shape))


class Items:
    def __init__(self, size, total, odd, even):
        self.size, self.total, self.at = size, total, Rows(total)
        self.slots = {step: odd if step % 2 else even for step in range(1, size)}
        self.first, self.count = {}, 0
        for step in range(1, size):
            self.first[step] = self.count
            self.count += self.slots[step]
        self.rows = {step: -(-(self.slots[step] + self.count) // 8) * 8 for step in self.slots}


def item_pack_kernel(items, place, plan, query, grad, *outs):
    size = items.size
    position = place[0]
    features = outs[0].shape[-1]
    for step in range(1, size):
        pair = position * size + lax.rem(position + step, size)
        tally = plan[items.at.tallies, pair]
        for slot in range(items.slots[step]):
            head = jnp.where(slot < tally, plan[items.at.lists + slot, pair], 0)
            columns = columns_of(head, features)
            outs[step - 1][slot, 0] = query[0, :, columns]
            outs[step - 1][slot, 1] = grad[0, :, columns]


def item_pack(items, place, plan, query, grad):
    tokens = query.shape[1]
    features = query.shape[2] // items.total
    return pl.pallas_call(
        functools.partial(item_pack_kernel, items),
        out_shape=[
            jax.ShapeDtypeStruct((items.slots[step], 2, tokens, features), jnp.bfloat16)
            for step in range(1, items.size)
        ],
        in_specs=[SMEM] * 2 + [VMEM] * 2,
        out_specs=[VMEM] * (items.size - 1),
        compiler_params=PARAMS,
        name="item_pack",
    )(place, plan, query, grad)


def each_item(items, position, plan):
    for step in range(1, items.size):
        origin = lax.rem(position + items.size - step, items.size)
        pair = origin * items.size + position
        tally = plan[items.at.tallies, pair]
        for slot in range(items.slots[step]):
            real = slot < tally
            head = jnp.where(real, plan[items.at.lists + slot, pair], 0)
            weight = jnp.where(real, plan[head, pair], 0).astype(jnp.float32)
            yield step, slot, head, weight


def columns_of(head, features):
    if isinstance(head, int):
        return pl.ds(head * features, features)
    return pl.ds(pl.multiple_of(head * features, features), features)


def by_groups(count, one, straight=8):
    straight = math.gcd(count, straight)

    def some(index, carry):
        for part in range(straight):
            one(index * straight + part)
        return carry

    lax.fori_loop(0, count // straight, some, 0)


def cost(blocks, products, side):
    return pl.CostEstimate(
        flops=2 * blocks * products * side**3,
        bytes_accessed=8 * blocks * side * side,
        transcendentals=blocks * side * side,
    )


def products(keys, values, queries, grads):
    factor = keys.shape[1] ** -0.5
    return dot(keys, queries, NT) * (factor * LOG2E), dot(values, grads, NT)


def one_total(scores, prob_grad):
    top = jnp.max(scores, axis=0, keepdims=True)
    exps = jnp.exp2(scores - top)
    total = jnp.sum(exps, axis=0, keepdims=True)
    moment = jnp.sum(exps * prob_grad, axis=0, keepdims=True)
    return top + jnp.log2(total), moment / total


def one_weight(scores, prob_grad, weight, log, delta):
    probs = jnp.exp2(scores - log) * weight
    return probs.astype(jnp.bfloat16), (probs * (prob_grad - delta)).astype(jnp.bfloat16)


def own_totals_kernel(total, query, key, value, grad, out, kept):
    features = query.shape[2] // total

    def one_head(head):
        columns = columns_of(head, features)
        block = [ref[0, :, columns] for ref in (key, value, query, grad)]
        scores, prob_grad = products(*block)
        kept[head, 0], kept[head, 1] = scores, prob_grad
        out[0, pl.ds(head, 1), :], out[1, pl.ds(head, 1), :] = one_total(scores, prob_grad)

    by_groups(total, one_head)


def run_own_totals(total, sources):
    tokens = sources[0].shape[1]
    return pl.pallas_call(
        functools.partial(own_totals_kernel, total),
        out_shape=[
            jax.ShapeDtypeStruct((2, total, tokens), jnp.float32),
            jax.ShapeDtypeStruct((total, 2, tokens, tokens), jnp.float32),
        ],
        in_specs=[VMEM] * 4,
        out_specs=[VMEM] * 2,
        compiler_params=PARAMS,
        cost_estimate=cost(total, 2, tokens),
        name="own_totals",
    )(*sources)


def totals_kernel(items, place, plan, key, value, own, *refs):
    size = items.size
    far_refs, (out, kept, *packets) = refs[: size - 1], refs[size - 1 :]
    position = place[0]
    features = key.shape[2] // items.total
    for step, packet in enumerate(packets, 1):
        pair = position * size + lax.rem(position + step, size)
        tally = plan[items.at.tallies, pair]
        for slot in range(items.slots[step]):
            head = jnp.where(slot < tally, plan[items.at.lists + slot, pair], 0)
            for plane in range(2):
                packet[plane, pl.ds(slot, 1), :] = own[plane, pl.ds(head, 1), :]
    for index, (step, slot, head, _) in enumerate(each_item(items, position, plan)):
        columns = columns_of(head, features)
        far = far_refs[step - 1]
        scores, prob_grad = products(key[0, :, columns], value[0, :, columns], far[slot, 0], far[slot, 1])
        kept[index, 0], kept[index, 1] = scores, prob_grad
        for plane, total in enumerate(one_total(scores, prob_grad)):
            out[plane, pl.ds(index, 1), :] = total
            for back, packet in enumerate(packets, 1):
                packet[plane, pl.ds(items.slots[back] + index, 1), :] = total


def run_totals(items, place, plan, sources, own, fars):
    tokens = sources[0].shape[1]
    rows = [-(-items.count // 8) * 8] + [items.rows[step] for step in range(1, items.size)]
    totals = [jax.ShapeDtypeStruct((2, count, tokens), jnp.float32) for count in rows]
    kept = jax.ShapeDtypeStruct((items.count, 2, tokens, tokens), jnp.float32)
    return pl.pallas_call(
        functools.partial(totals_kernel, items),
        out_shape=[totals[0], kept, *totals[1:]],
        in_specs=[SMEM] * 2 + [VMEM] * (2 + items.size),
        out_specs=[VMEM] * (1 + items.size),
        compiler_params=PARAMS,
        cost_estimate=cost(items.count, 2, tokens),
        name="totals",
    )(place, plan, *sources[1:3], own, *fars)


def far_part(items, position, plan, back, head, origin, gap, slot=None):
    column = lax.rem(position + items.size - back, items.size)
    entry = origin * items.size + column
    weight = plan[head, entry].astype(jnp.float32)
    if gap == 0:
        return weight, back, slot
    row = jnp.minimum(plan[items.at.slots + head, entry], items.slots[gap] - 1)
    return weight, back, items.slots[back] + items.first[gap] + row


def join(rows, totals, logs, means, shares, joined):
    for index, parts in enumerate(rows):
        at = pl.ds(index, 1)
        for part, (weight, back, row) in enumerate(parts):
            log = totals[back][0, pl.ds(row, 1), :]
            logs[part, at, :] = jnp.where(weight > 0, log, -jnp.inf)
            means[part, at, :] = totals[back][1, pl.ds(row, 1), :]
            shares[part, at, :] = jnp.broadcast_to(weight, log.shape)
    count = logs.shape[0]
    top = functools.reduce(jnp.maximum, [logs[part] for part in range(count)])
    weights = [shares[part] * jnp.exp2(logs[part] - top) for part in range(count)]
    total = sum(weights)
    joined[0] = top + jnp.log2(total)
    joined[1] = sum(weight * means[part] for part, weight in enumerate(weights)) / total


def join_scratch(items, count, tokens):
    rows = -(-count // 8) * 8
    part = pltpu.VMEM((items.size, rows, tokens), jnp.float32)
    return [part, part, part, pltpu.VMEM((2, rows, tokens), jnp.float32)]


def items_kernel(items, place, plan, key, kept, *refs):
    size = items.size
    totals, refs = refs[:size], refs[-4 - size :]
    made, item_outs, scratch = refs[0], refs[1:size], refs[size:]
    position = place[0]
    features = key.shape[2] // items.total
    factor = features**-0.5
    arrived = list(each_item(items, position, plan))
    rows = []
    for index, (step, slot, head, weight) in enumerate(arrived):
        origin = lax.rem(position + size - step, size)
        parts = [(weight, 0, index)]
        for back in range(1, size):
            gap = (step - back) % size
            parts.append(far_part(items, position, plan, back, head, origin, gap, slot))
        rows.append(parts)
    join(rows, totals, *scratch)
    joined = scratch[-1]
    for index, (step, slot, head, weight) in enumerate(arrived):
        log, delta = joined[0, pl.ds(index, 1), :], joined[1, pl.ds(index, 1), :]
        log = jnp.where(weight > 0, log, jnp.inf)
        probs, score_grad = one_weight(kept[index, 0], kept[index, 1], weight, log, delta)
        made[index, 0], made[index, 1] = probs, score_grad
        query_term = dot(score_grad, key[0, :, columns_of(head, features)], TN) * factor
        item_outs[step - 1][slot] = query_term.astype(jnp.bfloat16)


def run_items(items, place, plan, sources, kept, totals, after):
    _, tokens, width = sources[0].shape
    features = width // items.total
    outs = [jax.ShapeDtypeStruct(kept.shape, jnp.bfloat16)]
    for step in range(1, items.size):
        outs.append(jax.ShapeDtypeStruct((items.slots[step], tokens, features), jnp.bfloat16))
    return pl.pallas_call(
        functools.partial(items_kernel, items),
        out_shape=outs,
        in_specs=[SMEM] * 2 + [VMEM] * (2 + items.size) + [ANY] * len(after),
        out_specs=[VMEM] * len(outs),
        scratch_shapes=join_scratch(items, items.count, tokens),
        compiler_params=PARAMS,
        cost_estimate=cost(items.count, 5, tokens),
        name="items",
    )(place, plan, sources[1], kept, *totals, *after)


def own_kernel(items, place, plan, query, key, grad, kept, *refs):
    size = items.size
    totals, fars, made = refs[:size], refs[size : 2 * size - 1], refs[2 * size - 1]
    query_out, key_out, value_out = refs[2 * size : 2 * size + 3]
    key_sum, value_sum, *scratch = refs[2 * size + 3 :]
    position = place[0]
    features = query.shape[2] // items.total
    factor = features**-0.5
    rows = []
    for head in range(items.total):
        parts = [(plan[head, position * size + position].astype(jnp.float32), 0, head)]
        for back in range(1, size):
            parts.append(far_part(items, position, plan, back, head, position, size - back))
        rows.append(parts)
    join(rows, totals, *scratch)
    joined = scratch[-1]

    def one_head(head):
        log, delta = joined[0, pl.ds(head, 1), :], joined[1, pl.ds(head, 1), :]
        weight = plan[head, position * size + position].astype(jnp.float32)
        probs, score_grad = one_weight(kept[head, 0], kept[head, 1], weight, log, delta)
        columns = columns_of(head, features)
        key_sum[head] = dot(score_grad, query[0, :, columns])
        value_sum[head] = dot(probs, grad[0, :, columns])
        query_out[head] = dot(score_grad, key[0, :, columns], TN) * factor

    by_groups(items.total, one_head)
    for index, (step, slot, head, weight) in enumerate(each_item(items, position, plan)):
        far = fars[step - 1]
        key_sum[head] += dot(made[index, 1], far[slot, 0])
        value_sum[head] += dot(made[index, 0], far[slot, 1])

    def one_sum(head):
        columns = columns_of(head, features)
        key_out[0, :, columns] = (key_sum[head] * factor).astype(jnp.bfloat16)
        value_out[0, :, columns] = value_sum[head].astype(jnp.bfloat16)

    by_groups(items.total, one_sum)


def run_own(items, place, plan, sources, kept, totals, fars, made):
    _, tokens, width = sources[0].shape
    features = width // items.total
    each = (items.total, tokens, features)
    query, key, _, grad = sources
    return pl.pallas_call(
        functools.partial(own_kernel, items),
        out_shape=[
            jax.ShapeDtypeStruct(each, jnp.float32),
            jax.ShapeDtypeStruct(query.shape, jnp.bfloat16),
            jax.ShapeDtypeStruct(query.shape, jnp.bfloat16),
        ],
        in_specs=[SMEM] * 2 + [VMEM] * (4 + 2 * items.size),
        out_specs=[VMEM] * 3,
        scratch_shapes=[pltpu.VMEM(each, jnp.float32)] * 2
        + join_scratch(items, items.total, tokens),
        compiler_params=PARAMS,
        cost_estimate=cost(items.total + items.count, 5, tokens),
        name="own",
    )(place, plan, query, key, grad, kept, *totals, *fars, made)


def query_kernel(items, place, plan, own_query, *refs):
    size = items.size
    backs, (out, held, sems) = refs[: size - 1], refs[size - 1 :]
    position = place[0]
    features = own_query.shape[2]
    group = math.gcd(items.total, 4)

    def copy(first):
        columns = pl.ds(pl.multiple_of(first * features, 128), group * features)
        return pltpu.make_async_copy(held.at[:, columns], out.at[0, :, columns], sems.at[first // group])

    def some(index, carry):
        for part in range(group):
            head = index * group + part
            total = own_query[head]
            for step in range(1, size):
                entry = position * size + lax.rem(position + step, size)
                used = plan[head, entry] > 0
                slot = jnp.minimum(plan[items.at.slots + head, entry], items.slots[step] - 1)
                total += jnp.where(used, backs[step - 1][slot].astype(jnp.float32), 0.0)
            held[:, columns_of(head, features)] = total.astype(jnp.bfloat16)
        copy(index * group).start()
        return carry

    lax.fori_loop(0, items.total // group, some, 0)
    for first in range(0, items.total, group):
        copy(first).wait()


def query_gradient(items, place, plan, own_query, backs, shape):
    return pl.pallas_call(
        functools.partial(query_kernel, items),
        out_shape=jax.ShapeDtypeStruct(shape, jnp.bfloat16),
        in_specs=[SMEM] * 2 + [VMEM] * items.size,
        out_specs=ANY,
        scratch_shapes=[
            pltpu.VMEM(shape[1:], jnp.bfloat16),
            pltpu.SemaphoreType.DMA((items.total // math.gcd(items.total, 4),)),
        ],
        compiler_params=PARAMS,
        name="query_gradient",
    )(place, plan, own_query, *backs)


def shared_kernel(items, place, plan, *refs):
    size = items.size
    parts, outs, sems = refs[:size], refs[size + 3 : size + 6], refs[-1]
    position = place[0]
    features = parts[0].shape[2]
    copies = []
    for step in range(size):
        columns = columns_of(plan[items.at.shared, lax.rem(position + step, size)], features)
        for index, out in enumerate(outs):
            copies.append(
                pltpu.make_async_copy(
                    parts[step].at[index], out.at[0, :, columns], sems.at[step, index]
                )
            )
    for copy in copies:
        copy.start()
    for copy in copies:
        copy.wait()


def put_shared(items, place, plan, parts, grads):
    first = 2 + len(parts)
    return pl.pallas_call(
        functools.partial(shared_kernel, items),
        out_shape=[jax.ShapeDtypeStruct(grad.shape, jnp.bfloat16) for grad in grads],
        in_specs=[SMEM] * 2 + [VMEM] * len(parts) + [ANY] * 3,
        out_specs=[ANY] * 3,
        scratch_shapes=[pltpu.SemaphoreType.DMA((items.size, 3))],
        input_output_aliases={first + index: index for index in range(3)},
        compiler_params=PARAMS,
        name="put_shared",
    )(place, plan, *parts, *grads)


def items_plan(items, block, place, plan, sources):
    size = items.size
    width = sources[0].shape[2] // items.total
    packed = item_pack(items, place, plan, sources[0], sources[3])
    fars = [shift(packed[step - 1], step) for step in range(1, size)]
    shared_fars = send_group(size, width, items.at.shared, place, plan, sources, packed)
    own_totals, own_kept = run_own_totals(items.total, sources)
    totals, kept, *packets = run_totals(items, place, plan, sources, own_totals, fars)
    packets = [shift(packets[step - 1], step) for step in range(1, size)]
    made, *outs = run_items(items, place, plan, sources, kept, [totals, *packets], shared_fars)
    backs = [shift(outs[step - 1], -step) for step in range(1, size)]
    spot = plan[items.at.spot, :3]
    parts = run_heads(size, 1, block, spot, plan, sources, shared_fars, (made,))
    parts = [parts[0]] + [shift(parts[step], -step) for step in range(1, size)]
    own_query, *light = run_own(items, place, plan, sources, own_kept, [own_totals, *packets], fars, made)
    query_light = query_gradient(items, place, plan, own_query, backs, light[0].shape)
    return tuple(put_shared(items, place, plan, parts, (query_light, *light)))


def shards(query_states, key_states, value_states, out_grad, pattern, counts):
    size = lax.axis_size("seq")
    place = lax.axis_index("seq").astype(jnp.int32).reshape(1)
    heads, blocks, slots = pattern.shape
    block = query_states.shape[1] * size // blocks
    sources = (query_states, key_states, value_states, out_grad)

    def by_heads(*sources):
        uses = count_uses(pattern, counts)
        return dense_plan(size, heads, 1, block, place, uses, sources)

    if size > 4 or size % 2 or blocks != size or heads == 1:
        return by_heads(*sources)
    used = jnp.arange(slots, dtype=jnp.int32) < counts[:, :, None]
    named = jnp.where(used, pattern, size * blocks)
    parts = [named] + [shift(named, step) for step in range(1, size)]
    plan, choice = make_plan(size, heads, place, parts)

    def by_items(odd, even):
        items = Items(size, size * heads, odd, even)
        return lambda *sources: items_plan(items, block, place, plan, sources)

    branches = [by_items(odd, even) for odd, even in SIZES] + [by_heads]
    return lax.switch(choice[0], branches, *sources)


def solution(mesh):
    tokens = P(("groups", "mp", "rep"), "seq", None)
    return jax.shard_map(
        shards,
        mesh=mesh,
        in_specs=(tokens, tokens, tokens, tokens, P("seq", None, None), P("seq", None)),
        out_specs=(tokens, tokens, tokens),
        check_vma=False,
    )
```

profile of v0, /device:TPU:0, one launch (start us, length us, event | category | flops | bytes accessed | tf_op | source)
XLA Modules:
  0.0 87.2 jit_solution(638043083786713314)
XLA Ops:
  0.6 0.8 fusion.refs_0_
  1.4 3.0 %collective-permute-start.81 = (s32[4,4,6]{2,1,0:T(4,128)S(1)}, s32[4,4,6]{2,1,0:T(4,128)S(1)}, u32[]{:S(2)}, u32[]{:S(2)}) collective-permute-start(s32[4,4,6]{2,1,0:T(4,128)S(1)} %fusion.refs_0_), channel_id=1, source_target_pairs={{0,4},{4,8},{8,12},{12,0},{1,5},{5,9},{9,13},{13,1},{2,6},{6,10},{... | collective-permute-start | bytes 1160 | tf_op jit(solution)/shard_map/ppermute | solution.py:30
  4.4 2.6 %collective-permute-start.82 = (s32[4,4,6]{2,1,0:T(4,128)S(1)}, s32[4,4,6]{2,1,0:T(4,128)S(1)}, u32[]{:S(2)}, u32[]{:S(2)}) collective-permute-start(s32[4,4,6]{2,1,0:T(4,128)S(1)} %fusion.refs_0_), channel_id=1, source_target_pairs={{0,8},{4,12},{8,0},{12,4},{1,9},{5,13},{9,1},{13,5},{2,10},{6,14},... | collective-permute-start | bytes 1160 | tf_op jit(solution)/shard_map/ppermute | solution.py:30
  7.0 1.3 %collective-permute-start.83 = (s32[4,4,6]{2,1,0:T(4,128)S(1)}, s32[4,4,6]{2,1,0:T(4,128)S(1)}, u32[]{:S(2)}, u32[]{:S(2)}) collective-permute-start(s32[4,4,6]{2,1,0:T(4,128)S(1)} %fusion.refs_0_), channel_id=1, source_target_pairs={{0,12},{4,0},{8,4},{12,8},{1,13},{5,1},{9,5},{13,9},{2,14},{6,2},{... | collective-permute-start | bytes 1160 | tf_op jit(solution)/shard_map/ppermute | solution.py:30
  8.4 0.0 collective-permute-done.81.refs_1_
  8.4 0.7 collective-permute-done.82.refs_2_
  9.1 1.6 %collective-permute-done.83.refs_3_ = s32[4,4,6]{2,1,0:T(4,128)S(1)} collective-permute-done((s32[4,4,6]{2,1,0:T(4,128)S(1)}, s32[4,4,6]{2,1,0:T(4,128)S(1)}, u32[]{:S(2)}, u32[]{:S(2)}) %collective-permute-start.83) | collective-permute-done | bytes 416 | tf_op jit(solution)/shard_map/ppermute | solution.py:30
  10.7 1.4 %make_plan.1 = (s32[40,16]{1,0:T(8,128)S(1)}, s32[1]{0:T(128)}) custom-call(s32[1]{0:T(128)} %bitcast.5.place, s32[4,4,6]{2,1,0:T(4,128)S(1)} %fusion.refs_0_, s32[4,4,6]{2,1,0:T(4,128)S(1)} %collective-permute-done.81.refs_1_, s32[4,4,6]{2,1,0:T(4,128)S(1)} %collective-permute-done.82.refs_2_, s32[4,4,6]{2,1,0:T(4,128)S(1)} %collective-permute-done.83.refs_3_), custom_call_target="tpu_custom_call" | custom-call | tf_op jit(solution)/shard_map/make_plan/pallas_call | solution.py:138
  12.7 74.2 %conditional.1 = ((bf16[1,128,2048]{2,1,0:T(8,128)(2,1)}, bf16[1,128,2048]{2,1,0:T(8,128)(2,1)}, bf16[1,128,2048]{2,1,0:T(8,128)(2,1)})) conditional(s32[]{:T(128)} %bitcast.6, (s32[40,16]{1,0:T(8,128)S(1)}, s32[1]{0:T(128)}, bf16[1,128,2048]{2,1,0:T(8,128)(2,1)}, bf16[1,128,2048]{2,1,0:T(8,128)(2,1)}, ...), branch_computations={%region_0.1_spmd, %region_1.2_spmd, %region_2.3_spmd, %region_3.4_... | conditional | flops 1560281088 | bytes 28345064 | solution.py:807
  13.0 0.0 copy-start.5
  13.0 0.0 copy-start.10
  13.0 0.0 copy-start.15
  13.0 0.0 copy-start.20
  13.0 1.6 %item_pack.9 = (bf16[5,2,128,128]{3,2,1,0:T(8,128)(2,1)S(1)}, bf16[5,2,128,128]{3,2,1,0:T(8,128)(2,1)S(1)}, bf16[5,2,128,128]{3,2,1,0:T(8,128)(2,1)S(1)}) custom-call(s32[1]{0:T(128)} %get-tuple-element.194.place, s32[40,16]{1,0:T(8,128)S(1)} %get-tuple-element.195.plan.starts.uses, bf16[1,128,2048]{2,1,0:T(8,128)(2,1)} %get-tuple-element.196.query.refs_0_, ...), custom_call_target="tpu_custom_call" | custom-call | tf_op jit(solution)/shard_map/cond/branch_4_fun/item_pack/pallas_call | solution.py:412
  14.7 0.1 collective-permute-start.63
  14.8 3.6 %collective-permute-start.64 = (bf16[5,2,128,128]{3,2,1,0:T(8,128)(2,1)S(1)}, bf16[5,2,128,128]{3,2,1,0:T(8,128)(2,1)S(1)}, u32[]{:S(2)}, u32[]{:S(2)}) collective-permute-start(bf16[5,2,128,128]{3,2,1,0:T(8,128)(2,1)S(1)} %get-tuple-element.201.refs_5_), channel_id=1, source_target_pairs={{0,8},{4,12},{8,0},{12,4},{1,9},{5,13},{9,1},{13,5},{2,10},{6,14},... | collective-permute-start | bytes 983048 | tf_op jit(solution)/shard_map/cond/branch_4_fun/ppermute | solution.py:30
  18.4 0.1 collective-permute-start.65
  18.5 2.3 %pack.10 = (bf16[4,128,128]{2,1,0:T(8,128)(2,1)S(1)}, bf16[4,128,128]{2,1,0:T(8,128)(2,1)S(1)}, bf16[4,128,128]{2,1,0:T(8,128)(2,1)S(1)}) custom-call(s32[1]{0:T(128)} %get-tuple-element.194.place, s32[40,16]{1,0:T(8,128)S(1)} %get-tuple-element.195.plan.starts.uses, bf16[1,128,2048]{2,1,0:T(8,128)(2,1)} %get-tuple-element.196.query.refs_0_, ...), custom_call_target="tpu_custom_call" | custom-call | tf_op jit(solution)/shard_map/cond/branch_4_fun/pack/pallas_call | solution.py:180
  20.9 2.0 %collective-permute-start.60 = (bf16[4,128,128]{2,1,0:T(8,128)(2,1)S(1)}, bf16[4,128,128]{2,1,0:T(8,128)(2,1)S(1)}, u32[]{:S(2)}, u32[]{:S(2)}) collective-permute-start(bf16[4,128,128]{2,1,0:T(8,128)(2,1)S(1)} %get-tuple-element.203), channel_id=1, source_target_pairs={{0,4},{4,8},{8,12},{12,0},{1,5},{5,9},{9,13},{13,1},{2,6},{6,10},{... | collective-permute-start | bytes 393224 | tf_op jit(solution)/shard_map/cond/branch_4_fun/ppermute | solution.py:30
  22.8 0.2 collective-permute-start.61
  23.0 4.2 %collective-permute-done.63.refs_0_.refs_4_ = bf16[5,2,128,128]{3,2,1,0:T(8,128)(2,1)S(1)} collective-permute-done((bf16[5,2,128,128]{3,2,1,0:T(8,128)(2,1)S(1)}, bf16[5,2,128,128]{3,2,1,0:T(8,128)(2,1)S(1)}, u32[]{:S(2)}, u32[]{:S(2)}) %collective-permute-start.63) | collective-permute-done | bytes 327712 | tf_op jit(solution)/shard_map/cond/branch_4_fun/ppermute | solution.py:30
  27.3 1.3 %collective-permute-start.62 = (bf16[4,128,128]{2,1,0:T(8,128)(2,1)S(1)}, bf16[4,128,128]{2,1,0:T(8,128)(2,1)S(1)}, u32[]{:S(2)}, u32[]{:S(2)}) collective-permute-start(bf16[4,128,128]{2,1,0:T(8,128)(2,1)S(1)} %get-tuple-element.205), channel_id=1, source_target_pairs={{0,12},{4,0},{8,4},{12,8},{1,13},{5,1},{9,5},{13,9},{2,14},{6,2},{... | collective-permute-start | bytes 393224 | tf_op jit(solution)/shard_map/cond/branch_4_fun/ppermute | solution.py:30
  28.5 1.1 %own_totals.9 = (f32[2,16,128]{2,1,0:T(8,128)S(1)}, f32[16,2,128,128]{3,2,1,0:T(8,128)S(1)}) custom-call(bf16[1,128,2048]{2,1,0:T(8,128)(2,1)S(1)} %copy-done.10, bf16[1,128,2048]{2,1,0:T(8,128)(2,1)S(1)} %copy-done.5, bf16[1,128,2048]{2,1,0:T(8,128)(2,1)S(1)} %copy-done.20, bf16[1,128,2048]{2,1,0:T(8,128)(2,1)S(1)} %copy-done.15), custom_call_target="tpu_custom_call" | custom-call | flops 134217728 | bytes 2097152 | tf_op jit(solution)/shard_map/cond/branch_4_fun/own_totals/pallas_call | solution.py:495
  29.6 12.4 %collective-permute-done.64.refs_1_.refs_5_ = bf16[5,2,128,128]{3,2,1,0:T(8,128)(2,1)S(1)} collective-permute-done((bf16[5,2,128,128]{3,2,1,0:T(8,128)(2,1)S(1)}, bf16[5,2,128,128]{3,2,1,0:T(8,128)(2,1)S(1)}, u32[]{:S(2)}, u32[]{:S(2)}) %collective-permute-start.64) | collective-permute-done | bytes 327712 | tf_op jit(solution)/shard_map/cond/branch_4_fun/ppermute | solution.py:30
  42.1 0.0 collective-permute-done.65.refs_2_.refs_6_
  42.1 1.7 %totals.9 = (f32[2,16,128]{2,1,0:T(8,128)S(1)}, f32[15,2,128,128]{3,2,1,0:T(8,128)S(1)}, f32[2,24,128]{2,1,0:T(8,128)S(1)}, f32[2,24,128]{2,1,0:T(8,128)S(1)}, f32[2,24,128]{2,1,0:T(8,128)S(1)}) custom-call(s32[1]{0:T(128)} %get-tuple-element.194.place, s32[40,16]{1,0:T(8,128)S(1)} %get-tuple-element.195.plan.starts.uses, ...), custom_call_target="tpu_custom_call" | custom-call | flops 125829120 | bytes 1966080 | tf_op jit(solution)/shard_map/cond/branch_4_fun/totals/pallas_call | solution.py:537
  43.8 10.3 %collective-permute-start.66 = (f32[2,24,128]{2,1,0:T(8,128)S(1)}, f32[2,24,128]{2,1,0:T(8,128)S(1)}, u32[]{:S(2)}, u32[]{:S(2)}) collective-permute-start(f32[2,24,128]{2,1,0:T(8,128)S(1)} %get-tuple-element.209), channel_id=1, source_target_pairs={{0,4},{4,8},{8,12},{12,0},{1,5},{5,9},{9,13},{13,1},{2,6},{6,10},{... | collective-permute-start | bytes 73736 | tf_op jit(solution)/shard_map/cond/branch_4_fun/ppermute | solution.py:30
  54.1 2.1 %collective-permute-start.67 = (f32[2,24,128]{2,1,0:T(8,128)S(1)}, f32[2,24,128]{2,1,0:T(8,128)S(1)}, u32[]{:S(2)}, u32[]{:S(2)}) collective-permute-start(f32[2,24,128]{2,1,0:T(8,128)S(1)} %get-tuple-element.210), channel_id=1, source_target_pairs={{0,8},{4,12},{8,0},{12,4},{1,9},{5,13},{9,1},{13,5},{2,10},{6,14},... | collective-permute-start | bytes 73736 | tf_op jit(solution)/shard_map/cond/branch_4_fun/ppermute | solution.py:30
  56.2 0.3 collective-permute-start.68
  56.5 0.0 collective-permute-done.61.refs_5_
  56.5 0.0 collective-permute-done.62.refs_6_
  56.5 1.1 %collective-permute-done.66.refs_1_ = f32[2,24,128]{2,1,0:T(8,128)S(1)} collective-permute-done((f32[2,24,128]{2,1,0:T(8,128)S(1)}, f32[2,24,128]{2,1,0:T(8,128)S(1)}, u32[]{:S(2)}, u32[]{:S(2)}) %collective-permute-start.66) | collective-permute-done | bytes 24608 | tf_op jit(solution)/shard_map/cond/branch_4_fun/ppermute | solution.py:30
  57.7 1.1 %collective-permute-done.67.refs_2_ = f32[2,24,128]{2,1,0:T(8,128)S(1)} collective-permute-done((f32[2,24,128]{2,1,0:T(8,128)S(1)}, f32[2,24,128]{2,1,0:T(8,128)S(1)}, u32[]{:S(2)}, u32[]{:S(2)}) %collective-permute-start.67) | collective-permute-done | bytes 24608 | tf_op jit(solution)/shard_map/cond/branch_4_fun/ppermute | solution.py:30
  58.8 1.2 %collective-permute-done.68.refs_3_ = f32[2,24,128]{2,1,0:T(8,128)S(1)} collective-permute-done((f32[2,24,128]{2,1,0:T(8,128)S(1)}, f32[2,24,128]{2,1,0:T(8,128)S(1)}, u32[]{:S(2)}, u32[]{:S(2)}) %collective-permute-start.68) | collective-permute-done | bytes 24608 | tf_op jit(solution)/shard_map/cond/branch_4_fun/ppermute | solution.py:30
  60.0 1.6 %items.9 = (bf16[15,2,128,128]{3,2,1,0:T(8,128)(2,1)S(1)}, bf16[5,128,128]{2,1,0:T(8,128)(2,1)S(1)}, bf16[5,128,128]{2,1,0:T(8,128)(2,1)S(1)}, bf16[5,128,128]{2,1,0:T(8,128)(2,1)S(1)}) custom-call(s32[1]{0:T(128)} %get-tuple-element.194.place, s32[40,16]{1,0:T(8,128)S(1)} %get-tuple-element.195.plan.starts.uses, bf16[1,128,2048]{2,1,0:T(8,128)(2,1)S(1)} %copy-done.5, ...), custom_call_target="tpu_custom_call" | custom-call | flops 314572800 | bytes 1966080 | tf_op jit(solution)/shard_map/cond/branch_4_fun/items/pallas_call | solution.py:613
  61.7 2.2 %collective-permute-start.72 = (bf16[5,128,128]{2,1,0:T(8,128)(2,1)S(1)}, bf16[5,128,128]{2,1,0:T(8,128)(2,1)S(1)}, u32[]{:S(2)}, u32[]{:S(2)}) collective-permute-start(bf16[5,128,128]{2,1,0:T(8,128)(2,1)S(1)} %get-tuple-element.219), channel_id=1, source_target_pairs={{0,12},{4,0},{8,4},{12,8},{1,13},{5,1},{9,5},{13,9},{2,14},{6,2},{... | collective-permute-start | bytes 491528 | tf_op jit(solution)/shard_map/cond/branch_4_fun/ppermute | solution.py:30
  63.9 0.8 collective-permute-start.74
  64.6 2.9 %heads.10 = (bf16[3,128,128]{2,1,0:T(8,128)(2,1)S(1)}, bf16[3,128,128]{2,1,0:T(8,128)(2,1)S(1)}, bf16[3,128,128]{2,1,0:T(8,128)(2,1)S(1)}, bf16[3,128,128]{2,1,0:T(8,128)(2,1)S(1)}) custom-call(s32[3]{0:T(128)S(1)} %slice_bitcast_fusion.4.spot, s32[40,16]{1,0:T(8,128)S(1)} %get-tuple-element.195.plan.starts.uses, bf16[1,128,2048]{2,1,0:T(8,128)(2,1)S(1)} %copy-done.10, ...), custom_call_target="tpu_custom_call" | custom-call | flops 335544320 | bytes 917504 | tf_op jit(solution)/shard_map/cond/branch_4_fun/heads/pallas_call | solution.py:285
  67.5 3.1 %collective-permute-start.69 = (bf16[3,128,128]{2,1,0:T(8,128)(2,1)S(1)}, bf16[3,128,128]{2,1,0:T(8,128)(2,1)S(1)}, u32[]{:S(2)}, u32[]{:S(2)}) collective-permute-start(bf16[3,128,128]{2,1,0:T(8,128)(2,1)S(1)} %get-tuple-element.214), channel_id=1, source_target_pairs={{0,12},{4,0},{8,4},{12,8},{1,13},{5,1},{9,5},{13,9},{2,14},{6,2},{... | collective-permute-start | bytes 294920 | tf_op jit(solution)/shard_map/cond/branch_4_fun/ppermute | solution.py:30
  70.6 1.1 %collective-permute-start.70 = (bf16[3,128,128]{2,1,0:T(8,128)(2,1)S(1)}, bf16[3,128,128]{2,1,0:T(8,128)(2,1)S(1)}, u32[]{:S(2)}, u32[]{:S(2)}) collective-permute-start(bf16[3,128,128]{2,1,0:T(8,128)(2,1)S(1)} %get-tuple-element.215), channel_id=1, source_target_pairs={{0,8},{4,12},{8,0},{12,4},{1,9},{5,13},{9,1},{13,5},{2,10},{6,14},... | collective-permute-start | bytes 294920 | tf_op jit(solution)/shard_map/cond/branch_4_fun/ppermute | solution.py:30
  71.7 0.0 collective-permute-done.72.refs_0_
  71.7 5.5 %collective-permute-start.71 = (bf16[3,128,128]{2,1,0:T(8,128)(2,1)S(1)}, bf16[3,128,128]{2,1,0:T(8,128)(2,1)S(1)}, u32[]{:S(2)}, u32[]{:S(2)}) collective-permute-start(bf16[3,128,128]{2,1,0:T(8,128)(2,1)S(1)} %get-tuple-element.216), channel_id=1, source_target_pairs={{0,4},{4,8},{8,12},{12,0},{1,5},{5,9},{9,13},{13,1},{2,6},{6,10},{... | collective-permute-start | bytes 294920 | tf_op jit(solution)/shard_map/cond/branch_4_fun/ppermute | solution.py:30
  77.2 3.8 %own.9 = (f32[16,128,128]{2,1,0:T(8,128)S(1)}, bf16[1,128,2048]{2,1,0:T(8,128)(2,1)}, bf16[1,128,2048]{2,1,0:T(8,128)(2,1)}) custom-call(s32[1]{0:T(128)} %get-tuple-element.194.place, s32[40,16]{1,0:T(8,128)S(1)} %get-tuple-element.195.plan.starts.uses, bf16[1,128,2048]{2,1,0:T(8,128)(2,1)S(1)} %copy-done.10, bf16[1,128,2048]{2,1,0:T(8,128)(2,1)S(1)} %copy-done.5, ...), custom_call_target="tpu_custom_call" | custom-call | flops 650117120 | bytes 4063232 | tf_op jit(solution)/shard_map/cond/branch_4_fun/own/pallas_call | solution.py:670
  80.9 1.3 %collective-permute-done.73.refs_1_ = bf16[5,128,128]{2,1,0:T(8,128)(2,1)S(1)} collective-permute-done((bf16[5,128,128]{2,1,0:T(8,128)(2,1)S(1)}, bf16[5,128,128]{2,1,0:T(8,128)(2,1)S(1)}, u32[]{:S(2)}, u32[]{:S(2)}) %collective-permute-start.73) | collective-permute-done | bytes 163872 | tf_op jit(solution)/shard_map/cond/branch_4_fun/ppermute | solution.py:30
  82.2 2.0 %query_gradient.9.refs_4_ = bf16[1,128,2048]{2,1,0:T(8,128)(2,1)} custom-call(s32[1]{0:T(128)} %get-tuple-element.194.place, s32[40,16]{1,0:T(8,128)S(1)} %get-tuple-element.195.plan.starts.uses, f32[16,128,128]{2,1,0:T(8,128)S(1)} %get-tuple-element.218.own_query, bf16[5,128,128]{2,1,0:T(8,128)(2,1)S(1)} %collective-permute-done.72.refs_0_, ...), custom_call_target="tpu_custom_call" | custom-call | tf_op jit(solution)/shard_map/cond/branch_4_fun/query_gradient/pallas_call | solution.py:717
  84.3 0.0 collective-permute-done.69.refs_1_
  84.3 0.4 collective-permute-done.70.refs_2_
  84.7 1.7 %put_shared.9 = (bf16[1,128,2048]{2,1,0:T(8,128)(2,1)}, bf16[1,128,2048]{2,1,0:T(8,128)(2,1)}, bf16[1,128,2048]{2,1,0:T(8,128)(2,1)}) custom-call(s32[1]{0:T(128)} %get-tuple-element.194.place, s32[40,16]{1,0:T(8,128)S(1)} %get-tuple-element.195.plan.starts.uses, ...), custom_call_target="tpu_custom_call", output_to_operand_aliasing={{0}: (6, {}), {1}: (7, {}), {2}: (8, {})} | custom-call | tf_op jit(solution)/shard_map/cond/branch_4_fun/put_shared/pallas_call | solution.py:753
  (9 shorter events, 0.0 us)
Async XLA Ops:
  1.4 7.0 %collective-permute-start.81 = (s32[4,4,6]{2,1,0:T(4,128)S(1)}, s32[4,4,6]{2,1,0:T(4,128)S(1)}, u32[]{:S(2)}, u32[]{:S(2)}) collective-permute-start(s32[4,4,6]{2,1,0:T(4,128)S(1)} %fusion.refs_0_), channel_id=1, source_target_pairs={{0,4},{4,8},{8,12},{12,0},{1,5},{5,9},{9,13},{13,1},{2,6},{6,10},{... | collective-permute-start | bytes 1160 | tf_op jit(solution)/shard_map/ppermute | solution.py:30
  4.4 4.6 %collective-permute-start.82 = (s32[4,4,6]{2,1,0:T(4,128)S(1)}, s32[4,4,6]{2,1,0:T(4,128)S(1)}, u32[]{:S(2)}, u32[]{:S(2)}) collective-permute-start(s32[4,4,6]{2,1,0:T(4,128)S(1)} %fusion.refs_0_), channel_id=1, source_target_pairs={{0,8},{4,12},{8,0},{12,4},{1,9},{5,13},{9,1},{13,5},{2,10},{6,14},... | collective-permute-start | bytes 1160 | tf_op jit(solution)/shard_map/ppermute | solution.py:30
  7.0 3.7 %collective-permute-start.83 = (s32[4,4,6]{2,1,0:T(4,128)S(1)}, s32[4,4,6]{2,1,0:T(4,128)S(1)}, u32[]{:S(2)}, u32[]{:S(2)}) collective-permute-start(s32[4,4,6]{2,1,0:T(4,128)S(1)} %fusion.refs_0_), channel_id=1, source_target_pairs={{0,12},{4,0},{8,4},{12,8},{1,13},{5,1},{9,5},{13,9},{2,14},{6,2},{... | collective-permute-start | bytes 1160 | tf_op jit(solution)/shard_map/ppermute | solution.py:30
  13.0 15.5 %copy-start.5 = (bf16[1,128,2048]{2,1,0:T(8,128)(2,1)S(1)}, bf16[1,128,2048]{2,1,0:T(8,128)(2,1)}, u32[]{:S(2)}) copy-start(bf16[1,128,2048]{2,1,0:T(8,128)(2,1)} %get-tuple-element.197.refs_1_.key) | copy-start | bytes 1572868 | tf_op jit(solution)/shard_map/cond
  13.0 15.5 %copy-start.10 = (bf16[1,128,2048]{2,1,0:T(8,128)(2,1)S(1)}, bf16[1,128,2048]{2,1,0:T(8,128)(2,1)}, u32[]{:S(2)}) copy-start(bf16[1,128,2048]{2,1,0:T(8,128)(2,1)} %get-tuple-element.196.query.refs_0_) | copy-start | bytes 1572868 | tf_op jit(solution)/shard_map/cond
  13.0 15.5 %copy-start.15 = (bf16[1,128,2048]{2,1,0:T(8,128)(2,1)S(1)}, bf16[1,128,2048]{2,1,0:T(8,128)(2,1)}, u32[]{:S(2)}) copy-start(bf16[1,128,2048]{2,1,0:T(8,128)(2,1)} %get-tuple-element.199.grad.refs_3_) | copy-start | bytes 1572868 | tf_op jit(solution)/shard_map/cond
  13.0 15.5 %copy-start.20 = (bf16[1,128,2048]{2,1,0:T(8,128)(2,1)S(1)}, bf16[1,128,2048]{2,1,0:T(8,128)(2,1)}, u32[]{:S(2)}) copy-start(bf16[1,128,2048]{2,1,0:T(8,128)(2,1)} %get-tuple-element.198.refs_2_.value) | copy-start | bytes 1572868 | tf_op jit(solution)/shard_map/cond
  14.7 12.6 %collective-permute-start.63 = (bf16[5,2,128,128]{3,2,1,0:T(8,128)(2,1)S(1)}, bf16[5,2,128,128]{3,2,1,0:T(8,128)(2,1)S(1)}, u32[]{:S(2)}, u32[]{:S(2)}) collective-permute-start(bf16[5,2,128,128]{3,2,1,0:T(8,128)(2,1)S(1)} %get-tuple-element.200.refs_4_), channel_id=1, source_target_pairs={{0,4},{4,8},{8,12},{12,0},{1,5},{5,9},{9,13},{13,1},{2,6},{6,10},{... | collective-permute-start | bytes 983048 | tf_op jit(solution)/shard_map/cond/branch_4_fun/ppermute | solution.py:30
  14.8 27.3 %collective-permute-start.64 = (bf16[5,2,128,128]{3,2,1,0:T(8,128)(2,1)S(1)}, bf16[5,2,128,128]{3,2,1,0:T(8,128)(2,1)S(1)}, u32[]{:S(2)}, u32[]{:S(2)}) collective-permute-start(bf16[5,2,128,128]{3,2,1,0:T(8,128)(2,1)S(1)} %get-tuple-element.201.refs_5_), channel_id=1, source_target_pairs={{0,8},{4,12},{8,0},{12,4},{1,9},{5,13},{9,1},{13,5},{2,10},{6,14},... | collective-permute-start | bytes 983048 | tf_op jit(solution)/shard_map/cond/branch_4_fun/ppermute | solution.py:30
  18.4 23.6 %collective-permute-start.65 = (bf16[5,2,128,128]{3,2,1,0:T(8,128)(2,1)S(1)}, bf16[5,2,128,128]{3,2,1,0:T(8,128)(2,1)S(1)}, u32[]{:S(2)}, u32[]{:S(2)}) collective-permute-start(bf16[5,2,128,128]{3,2,1,0:T(8,128)(2,1)S(1)} %get-tuple-element.202.refs_6_), channel_id=1, source_target_pairs={{0,12},{4,0},{8,4},{12,8},{1,13},{5,1},{9,5},{13,9},{2,14},{6,2},{... | collective-permute-start | bytes 983048 | tf_op jit(solution)/shard_map/cond/branch_4_fun/ppermute | solution.py:30
  20.9 35.3 %collective-permute-start.60 = (bf16[4,128,128]{2,1,0:T(8,128)(2,1)S(1)}, bf16[4,128,128]{2,1,0:T(8,128)(2,1)S(1)}, u32[]{:S(2)}, u32[]{:S(2)}) collective-permute-start(bf16[4,128,128]{2,1,0:T(8,128)(2,1)S(1)} %get-tuple-element.203), channel_id=1, source_target_pairs={{0,4},{4,8},{8,12},{12,0},{1,5},{5,9},{9,13},{13,1},{2,6},{6,10},{... | collective-permute-start | bytes 393224 | tf_op jit(solution)/shard_map/cond/branch_4_fun/ppermute | solution.py:30
  22.8 33.7 %collective-permute-start.61 = (bf16[4,128,128]{2,1,0:T(8,128)(2,1)S(1)}, bf16[4,128,128]{2,1,0:T(8,128)(2,1)S(1)}, u32[]{:S(2)}, u32[]{:S(2)}) collective-permute-start(bf16[4,128,128]{2,1,0:T(8,128)(2,1)S(1)} %get-tuple-element.204), channel_id=1, source_target_pairs={{0,8},{4,12},{8,0},{12,4},{1,9},{5,13},{9,1},{13,5},{2,10},{6,14},... | collective-permute-start | bytes 393224 | tf_op jit(solution)/shard_map/cond/branch_4_fun/ppermute | solution.py:30
  27.3 29.3 %collective-permute-start.62 = (bf16[4,128,128]{2,1,0:T(8,128)(2,1)S(1)}, bf16[4,128,128]{2,1,0:T(8,128)(2,1)S(1)}, u32[]{:S(2)}, u32[]{:S(2)}) collective-permute-start(bf16[4,128,128]{2,1,0:T(8,128)(2,1)S(1)} %get-tuple-element.205), channel_id=1, source_target_pairs={{0,12},{4,0},{8,4},{12,8},{1,13},{5,1},{9,5},{13,9},{2,14},{6,2},{... | collective-permute-start | bytes 393224 | tf_op jit(solution)/shard_map/cond/branch_4_fun/ppermute | solution.py:30
  43.8 13.9 %collective-permute-start.66 = (f32[2,24,128]{2,1,0:T(8,128)S(1)}, f32[2,24,128]{2,1,0:T(8,128)S(1)}, u32[]{:S(2)}, u32[]{:S(2)}) collective-permute-start(f32[2,24,128]{2,1,0:T(8,128)S(1)} %get-tuple-element.209), channel_id=1, source_target_pairs={{0,4},{4,8},{8,12},{12,0},{1,5},{5,9},{9,13},{13,1},{2,6},{6,10},{... | collective-permute-start | bytes 73736 | tf_op jit(solution)/shard_map/cond/branch_4_fun/ppermute | solution.py:30
  54.1 4.7 %collective-permute-start.67 = (f32[2,24,128]{2,1,0:T(8,128)S(1)}, f32[2,24,128]{2,1,0:T(8,128)S(1)}, u32[]{:S(2)}, u32[]{:S(2)}) collective-permute-start(f32[2,24,128]{2,1,0:T(8,128)S(1)} %get-tuple-element.210), channel_id=1, source_target_pairs={{0,8},{4,12},{8,0},{12,4},{1,9},{5,13},{9,1},{13,5},{2,10},{6,14},... | collective-permute-start | bytes 73736 | tf_op jit(solution)/shard_map/cond/branch_4_fun/ppermute | solution.py:30
  56.2 3.8 %collective-permute-start.68 = (f32[2,24,128]{2,1,0:T(8,128)S(1)}, f32[2,24,128]{2,1,0:T(8,128)S(1)}, u32[]{:S(2)}, u32[]{:S(2)}) collective-permute-start(f32[2,24,128]{2,1,0:T(8,128)S(1)} %get-tuple-element.211), channel_id=1, source_target_pairs={{0,12},{4,0},{8,4},{12,8},{1,13},{5,1},{9,5},{13,9},{2,14},{6,2},{... | collective-permute-start | bytes 73736 | tf_op jit(solution)/shard_map/cond/branch_4_fun/ppermute | solution.py:30
  61.7 10.1 %collective-permute-start.72 = (bf16[5,128,128]{2,1,0:T(8,128)(2,1)S(1)}, bf16[5,128,128]{2,1,0:T(8,128)(2,1)S(1)}, u32[]{:S(2)}, u32[]{:S(2)}) collective-permute-start(bf16[5,128,128]{2,1,0:T(8,128)(2,1)S(1)} %get-tuple-element.219), channel_id=1, source_target_pairs={{0,12},{4,0},{8,4},{12,8},{1,13},{5,1},{9,5},{13,9},{2,14},{6,2},{... | collective-permute-start | bytes 491528 | tf_op jit(solution)/shard_map/cond/branch_4_fun/ppermute | solution.py:30
  63.9 18.4 %collective-permute-start.73 = (bf16[5,128,128]{2,1,0:T(8,128)(2,1)S(1)}, bf16[5,128,128]{2,1,0:T(8,128)(2,1)S(1)}, u32[]{:S(2)}, u32[]{:S(2)}) collective-permute-start(bf16[5,128,128]{2,1,0:T(8,128)(2,1)S(1)} %get-tuple-element.220), channel_id=1, source_target_pairs={{0,8},{4,12},{8,0},{12,4},{1,9},{5,13},{9,1},{13,5},{2,10},{6,14},... | collective-permute-start | bytes 491528 | tf_op jit(solution)/shard_map/cond/branch_4_fun/ppermute | solution.py:30
  63.9 18.4 %collective-permute-start.74 = (bf16[5,128,128]{2,1,0:T(8,128)(2,1)S(1)}, bf16[5,128,128]{2,1,0:T(8,128)(2,1)S(1)}, u32[]{:S(2)}, u32[]{:S(2)}) collective-permute-start(bf16[5,128,128]{2,1,0:T(8,128)(2,1)S(1)} %get-tuple-element.221), channel_id=1, source_target_pairs={{0,4},{4,8},{8,12},{12,0},{1,5},{5,9},{9,13},{13,1},{2,6},{6,10},{... | collective-permute-start | bytes 491528 | tf_op jit(solution)/shard_map/cond/branch_4_fun/ppermute | solution.py:30
  67.5 16.8 %collective-permute-start.69 = (bf16[3,128,128]{2,1,0:T(8,128)(2,1)S(1)}, bf16[3,128,128]{2,1,0:T(8,128)(2,1)S(1)}, u32[]{:S(2)}, u32[]{:S(2)}) collective-permute-start(bf16[3,128,128]{2,1,0:T(8,128)(2,1)S(1)} %get-tuple-element.214), channel_id=1, source_target_pairs={{0,12},{4,0},{8,4},{12,8},{1,13},{5,1},{9,5},{13,9},{2,14},{6,2},{... | collective-permute-start | bytes 294920 | tf_op jit(solution)/shard_map/cond/branch_4_fun/ppermute | solution.py:30
  70.6 14.1 %collective-permute-start.70 = (bf16[3,128,128]{2,1,0:T(8,128)(2,1)S(1)}, bf16[3,128,128]{2,1,0:T(8,128)(2,1)S(1)}, u32[]{:S(2)}, u32[]{:S(2)}) collective-permute-start(bf16[3,128,128]{2,1,0:T(8,128)(2,1)S(1)} %get-tuple-element.215), channel_id=1, source_target_pairs={{0,8},{4,12},{8,0},{12,4},{1,9},{5,13},{9,1},{13,5},{2,10},{6,14},... | collective-permute-start | bytes 294920 | tf_op jit(solution)/shard_map/cond/branch_4_fun/ppermute | solution.py:30
  71.7 12.9 %collective-permute-start.71 = (bf16[3,128,128]{2,1,0:T(8,128)(2,1)S(1)}, bf16[3,128,128]{2,1,0:T(8,128)(2,1)S(1)}, u32[]{:S(2)}, u32[]{:S(2)}) collective-permute-start(bf16[3,128,128]{2,1,0:T(8,128)(2,1)S(1)} %get-tuple-element.216), channel_id=1, source_target_pairs={{0,4},{4,8},{8,12},{12,0},{1,5},{5,9},{9,13},{13,1},{2,6},{6,10},{... | collective-permute-start | bytes 294920 | tf_op jit(solution)/shard_map/cond/branch_4_fun/ppermute | solution.py:30
where the time goes:
time: 87.4 us; the launch traced here: 87.2 us
  starting transfers between devices  39.6 us (45%)
  waiting for transfers between devices  24.1 us (28%)
  Pallas kernels  20.2 us (23%)
  between operations  1.51 us (2%)
  loops' own time  0.93 us (1%)
    ppermute x18, starting transfers between devices, shift(): lax.ppermute(array, 'seq', [(j, (j + step) % size) for j in range(size)])  39.6 us
    ppermute x18, waiting for transfers between devices, shift(): lax.ppermute(array, 'seq', [(j, (j + step) % size) for j in range(size)])  24.1 us
    pallas_call x1, Pallas kernels, run_own(): pl.pallas_call(functools.partial(own_kernel, items), out_shape=[jax.Shape...  3.75 us
    pallas_call x1, Pallas kernels, run_heads(): pl.pallas_call(functools.partial(heads_kernel, size, heads, block), grid_...  2.85 us
    pallas_call x1, Pallas kernels, pack(): pl.pallas_call(functools.partial(pack_kernel, size, width, row), out_shap...  2.33 us
    pallas_call x1, Pallas kernels, query_gradient(): pl.pallas_call(functools.partial(query_kernel, items), out_shape=jax.Shap...  2.05 us
  transfers between devices with their start and end apart: 18, of which 9 were waited for; matrix products, arithmetic and copies ran while one was open for 0% of the time, Pallas kernels for 16%

commit v1 on v0

--- a/solution.py
+++ b/solution.py
@@ -98,18 +98,22 @@
         uses = jnp.where(pair == block * (size + 1), 0.0, uses)
     lane = lax.broadcasted_iota(jnp.int32, (1, pairs), 1)
     shared, mine = jnp.zeros((1, pairs), jnp.int32), jnp.zeros((1, 1), jnp.int32)
+    odd = functools.reduce(
+        jnp.logical_or, [lane == i * size + j for i in range(size) for j in range(size) if (i - j) % 2]
+    )
     number = head[:, :1].astype(jnp.float32)
     free = number >= 0
     for index in range(size):
-        load = jnp.sum(uses, axis=0, keepdims=True)
-        score = jnp.sum(uses * (load * load * load), axis=1, keepdims=True)
-        score = jnp.where(free, score * total + number, -1.0)
+        load = jnp.sum(uses, axis=0, keepdims=True) + jnp.where(odd, 0.0, 0.6)
+        load = load * load * load
+        score = jnp.sum(uses * (load * load), axis=1, keepdims=True)
+        score = jnp.where(free, score, -1.0)
         top = jnp.max(score, axis=0, keepdims=True)
-        uses = jnp.where(score == top, 0.0, uses)
-        free = free & (score != top)
-        name = (top - total * jnp.floor(top * (1.0 / total))).astype(jnp.int32)
-        shared = jnp.where(lane == index, name, shared)
-        mine = jnp.where(index == position, name, mine)
+        name = jnp.max(jnp.where(score == top, number, -1.0), axis=0, keepdims=True)
+        uses = jnp.where(number == name, 0.0, uses)
+        free = free & (number != name)
+        shared = jnp.where(lane == index, name.astype(jnp.int32), shared)
+        mine = jnp.where(index == position, name.astype(jnp.int32), mine)
     earlier = lax.broadcasted_iota(jnp.int32, (total, total), 1) < lax.broadcasted_iota(jnp.int32, (total, total), 0)
     slots = dot(earlier.astype(jnp.float32), uses)
     tallies = jnp.sum(uses, axis=0, keepdims=True)
@@ -121,9 +125,6 @@
     plan[pl.ds(rows.shared, 1), :] = shared
     plan[pl.ds(rows.spot, 1), :] = jnp.where(lane == 0, position, mine)
 
-    odd = functools.reduce(
-        jnp.logical_or, [lane == i * size + j for i in range(size) for j in range(size) if (i - j) % 2]
-    )
     most_odd = jnp.max(jnp.where(odd, tallies, 0.0)).astype(jnp.int32)
     most_even = jnp.max(jnp.where(odd, 0.0, tallies)).astype(jnp.int32)
     chosen = jnp.int32(len(SIZES))

time: 87.4 us -> 68.7 us (0.79); the launches traced: 87.2 us -> 69.8 us
  waiting for transfers between devices: 24.1 us -> 15.6 us
  starting transfers between devices: 39.6 us -> 31.5 us
    ppermute x18, waiting for transfers between devices: 24.1 us -> 15.6 us  [shift(): lax.ppermute(array, 'seq', [(j, (j + step) % size) for j in range(size)])]
    ppermute x18, starting transfers between devices: 39.6 us -> 31.5 us  [shift(): lax.ppermute(array, 'seq', [(j, (j + step) % size) for j in range(size)])]
  transfers between devices with their start and end apart: 18 -> 18, of which waited for: 9 -> 8; matrix products, arithmetic and copies ran while one was open for 0% -> 0% of each run, Pallas kernels for 16% -> 19%
where the time goes in v1:
time: 68.7 us; the launch traced here: 69.8 us
  starting transfers between devices  31.5 us (46%)
  Pallas kernels  19.4 us (28%)
  waiting for transfers between devices  15.6 us (23%)
  between operations  1.51 us (2%)
  loops' own time  0.85 us (1%)
  other arithmetic  0.77 us (1%)
    ppermute x18, starting transfers between devices, shift(): lax.ppermute(array, 'seq', [(j, (j + step) % size) for j in range(size)])  31.5 us
    ppermute x18, waiting for transfers between devices, shift(): lax.ppermute(array, 'seq', [(j, (j + step) % size) for j in range(size)])  15.6 us
    pallas_call x1, Pallas kernels, run_own(): pl.pallas_call(functools.partial(own_kernel, items), out_shape=[jax.Shape...  3.59 us
    pallas_call x1, Pallas kernels, run_heads(): pl.pallas_call(functools.partial(heads_kernel, size, heads, block), grid_...  2.85 us
    pallas_call x1, Pallas kernels, pack(): pl.pallas_call(functools.partial(pack_kernel, size, width, row), out_shap...  2.33 us
    pallas_call x1, Pallas kernels, query_gradient(): pl.pallas_call(functools.partial(query_kernel, items), out_shape=jax.Shap...  2.05 us
    pallas_call x1, Pallas kernels, put_shared(): pl.pallas_call(functools.partial(shared_kernel, items), out_shape=[jax.Sh...  1.72 us
    pallas_call x1, Pallas kernels, item_pack(): pl.pallas_call(functools.partial(item_pack_kernel, items), out_shape=[jax...  1.52 us
  transfers between devices with their start and end apart: 18, of which 8 were waited for; matrix products, arithmetic and copies ran while one was open for 0% of the time, Pallas kernels for 19%

profile of v1, /device:TPU:0, one launch (start us, length us, event | category | flops | bytes accessed | tf_op | source)
XLA Modules:
  0.0 69.8 jit_solution(16858576595700382479)
XLA Ops:
  0.6 0.8 %fusion.refs_0_ = s32[4,4,6]{2,1,0:T(4,128)S(1)} fusion(s32[4,4,6]{2,1,0:T(4,128)} %param.16, s32[4,4]{1,0:T(4,128)} %param.17), kind=kLoop, calls=%fused_computation.7 | loop fusion | flops 192 | bytes 832 | tf_op jit(solution)/shard_map/jit(_where)/select_n | solution.py:799
  1.4 3.0 %collective-permute-start.81 = (s32[4,4,6]{2,1,0:T(4,128)S(1)}, s32[4,4,6]{2,1,0:T(4,128)S(1)}, u32[]{:S(2)}, u32[]{:S(2)}) collective-permute-start(s32[4,4,6]{2,1,0:T(4,128)S(1)} %fusion.refs_0_), channel_id=1, source_target_pairs={{0,4},{4,8},{8,12},{12,0},{1,5},{5,9},{9,13},{13,1},{2,6},{6,10},{... | collective-permute-start | bytes 1160 | tf_op jit(solution)/shard_map/ppermute | solution.py:30
  4.4 2.6 %collective-permute-start.82 = (s32[4,4,6]{2,1,0:T(4,128)S(1)}, s32[4,4,6]{2,1,0:T(4,128)S(1)}, u32[]{:S(2)}, u32[]{:S(2)}) collective-permute-start(s32[4,4,6]{2,1,0:T(4,128)S(1)} %fusion.refs_0_), channel_id=1, source_target_pairs={{0,8},{4,12},{8,0},{12,4},{1,9},{5,13},{9,1},{13,5},{2,10},{6,14},... | collective-permute-start | bytes 1160 | tf_op jit(solution)/shard_map/ppermute | solution.py:30
  7.0 1.3 %collective-permute-start.83 = (s32[4,4,6]{2,1,0:T(4,128)S(1)}, s32[4,4,6]{2,1,0:T(4,128)S(1)}, u32[]{:S(2)}, u32[]{:S(2)}) collective-permute-start(s32[4,4,6]{2,1,0:T(4,128)S(1)} %fusion.refs_0_), channel_id=1, source_target_pairs={{0,12},{4,0},{8,4},{12,8},{1,13},{5,1},{9,5},{13,9},{2,14},{6,2},{... | collective-permute-start | bytes 1160 | tf_op jit(solution)/shard_map/ppermute | solution.py:30
  8.4 0.7 collective-permute-done.82.refs_2_
  9.1 1.6 %collective-permute-done.83.refs_3_ = s32[4,4,6]{2,1,0:T(4,128)S(1)} collective-permute-done((s32[4,4,6]{2,1,0:T(4,128)S(1)}, s32[4,4,6]{2,1,0:T(4,128)S(1)}, u32[]{:S(2)}, u32[]{:S(2)}) %collective-permute-start.83) | collective-permute-done | bytes 416 | tf_op jit(solution)/shard_map/ppermute | solution.py:30
  10.7 1.4 %make_plan.1 = (s32[40,16]{1,0:T(8,128)S(1)}, s32[1]{0:T(128)}) custom-call(s32[1]{0:T(128)} %bitcast.5.place, s32[4,4,6]{2,1,0:T(4,128)S(1)} %fusion.refs_0_, s32[4,4,6]{2,1,0:T(4,128)S(1)} %collective-permute-done.81.refs_1_, s32[4,4,6]{2,1,0:T(4,128)S(1)} %collective-permute-done.82.refs_2_, s32[4,4,6]{2,1,0:T(4,128)S(1)} %collective-permute-done.83.refs_3_), custom_call_target="tpu_custom_call" | custom-call | tf_op jit(solution)/shard_map/make_plan/pallas_call | solution.py:139
  12.8 56.8 %conditional.1 = ((bf16[1,128,2048]{2,1,0:T(8,128)(2,1)}, bf16[1,128,2048]{2,1,0:T(8,128)(2,1)}, bf16[1,128,2048]{2,1,0:T(8,128)(2,1)})) conditional(s32[]{:T(128)} %bitcast.6, (s32[40,16]{1,0:T(8,128)S(1)}, s32[1]{0:T(128)}, bf16[1,128,2048]{2,1,0:T(8,128)(2,1)}, bf16[1,128,2048]{2,1,0:T(8,128)(2,1)}, ...), branch_computations={%region_0.1_spmd, %region_1.2_spmd, %region_2.3_spmd, %region_3.4_... | conditional | flops 1560281088 | bytes 28345064 | solution.py:808
  12.8 0.0 copy-start.2
  12.8 0.0 copy-start.7
  12.8 0.0 copy-start.12
  12.8 0.0 copy-start.17
  12.8 1.5 %item_pack.6 = (bf16[3,2,128,128]{3,2,1,0:T(8,128)(2,1)S(1)}, bf16[3,2,128,128]{3,2,1,0:T(8,128)(2,1)S(1)}, bf16[3,2,128,128]{3,2,1,0:T(8,128)(2,1)S(1)}) custom-call(s32[1]{0:T(128)} %get-tuple-element.104.place, s32[40,16]{1,0:T(8,128)S(1)} %get-tuple-element.105.plan.starts.uses, bf16[1,128,2048]{2,1,0:T(8,128)(2,1)} %get-tuple-element.106.query.refs_0_, ...), custom_call_target="tpu_custom_call" | custom-call | tf_op jit(solution)/shard_map/cond/branch_1_fun/item_pack/pallas_call | solution.py:413
  14.4 0.1 collective-permute-start.18
  14.5 3.6 %collective-permute-start.19 = (bf16[3,2,128,128]{3,2,1,0:T(8,128)(2,1)S(1)}, bf16[3,2,128,128]{3,2,1,0:T(8,128)(2,1)S(1)}, u32[]{:S(2)}, u32[]{:S(2)}) collective-permute-start(bf16[3,2,128,128]{3,2,1,0:T(8,128)(2,1)S(1)} %get-tuple-element.111.refs_5_), channel_id=1, source_target_pairs={{0,8},{4,12},{8,0},{12,4},{1,9},{5,13},{9,1},{13,5},{2,10},{6,14},... | collective-permute-start | bytes 589832 | tf_op jit(solution)/shard_map/cond/branch_1_fun/ppermute | solution.py:30
  18.1 0.1 collective-permute-start.20
  18.2 2.3 %pack.7 = (bf16[4,128,128]{2,1,0:T(8,128)(2,1)S(1)}, bf16[4,128,128]{2,1,0:T(8,128)(2,1)S(1)}, bf16[4,128,128]{2,1,0:T(8,128)(2,1)S(1)}) custom-call(s32[1]{0:T(128)} %get-tuple-element.104.place, s32[40,16]{1,0:T(8,128)S(1)} %get-tuple-element.105.plan.starts.uses, bf16[1,128,2048]{2,1,0:T(8,128)(2,1)} %get-tuple-element.106.query.refs_0_, ...), custom_call_target="tpu_custom_call" | custom-call | tf_op jit(solution)/shard_map/cond/branch_1_fun/pack/pallas_call | solution.py:181
  20.6 2.0 %collective-permute-start.15 = (bf16[4,128,128]{2,1,0:T(8,128)(2,1)S(1)}, bf16[4,128,128]{2,1,0:T(8,128)(2,1)S(1)}, u32[]{:S(2)}, u32[]{:S(2)}) collective-permute-start(bf16[4,128,128]{2,1,0:T(8,128)(2,1)S(1)} %get-tuple-element.113), channel_id=1, source_target_pairs={{0,4},{4,8},{8,12},{12,0},{1,5},{5,9},{9,13},{13,1},{2,6},{6,10},{... | collective-permute-start | bytes 393224 | tf_op jit(solution)/shard_map/cond/branch_1_fun/ppermute | solution.py:30
  22.5 0.2 collective-permute-start.16
  22.7 1.4 %collective-permute-done.18.refs_0_.refs_4_ = bf16[3,2,128,128]{3,2,1,0:T(8,128)(2,1)S(1)} collective-permute-done((bf16[3,2,128,128]{3,2,1,0:T(8,128)(2,1)S(1)}, bf16[3,2,128,128]{3,2,1,0:T(8,128)(2,1)S(1)}, u32[]{:S(2)}, u32[]{:S(2)}) %collective-permute-start.18) | collective-permute-done | bytes 196640 | tf_op jit(solution)/shard_map/cond/branch_1_fun/ppermute | solution.py:30
  24.1 1.5 %collective-permute-start.17 = (bf16[4,128,128]{2,1,0:T(8,128)(2,1)S(1)}, bf16[4,128,128]{2,1,0:T(8,128)(2,1)S(1)}, u32[]{:S(2)}, u32[]{:S(2)}) collective-permute-start(bf16[4,128,128]{2,1,0:T(8,128)(2,1)S(1)} %get-tuple-element.115), channel_id=1, source_target_pairs={{0,12},{4,0},{8,4},{12,8},{1,13},{5,1},{9,5},{13,9},{2,14},{6,2},{... | collective-permute-start | bytes 393224 | tf_op jit(solution)/shard_map/cond/branch_1_fun/ppermute | solution.py:30
  25.6 1.1 %own_totals.6 = (f32[2,16,128]{2,1,0:T(8,128)S(1)}, f32[16,2,128,128]{3,2,1,0:T(8,128)S(1)}) custom-call(bf16[1,128,2048]{2,1,0:T(8,128)(2,1)S(1)} %copy-done.7, bf16[1,128,2048]{2,1,0:T(8,128)(2,1)S(1)} %copy-done.2, bf16[1,128,2048]{2,1,0:T(8,128)(2,1)S(1)} %copy-done.17, bf16[1,128,2048]{2,1,0:T(8,128)(2,1)S(1)} %copy-done.12), custom_call_target="tpu_custom_call" | custom-call | flops 134217728 | bytes 2097152 | tf_op jit(solution)/shard_map/cond/branch_1_fun/own_totals/pallas_call | solution.py:496
  26.7 6.5 %collective-permute-done.19.refs_1_.refs_5_ = bf16[3,2,128,128]{3,2,1,0:T(8,128)(2,1)S(1)} collective-permute-done((bf16[3,2,128,128]{3,2,1,0:T(8,128)(2,1)S(1)}, bf16[3,2,128,128]{3,2,1,0:T(8,128)(2,1)S(1)}, u32[]{:S(2)}, u32[]{:S(2)}) %collective-permute-start.19) | collective-permute-done | bytes 196640 | tf_op jit(solution)/shard_map/cond/branch_1_fun/ppermute | solution.py:30
  33.2 1.4 %totals.6 = (f32[2,16,128]{2,1,0:T(8,128)S(1)}, f32[9,2,128,128]{3,2,1,0:T(8,128)S(1)}, f32[2,16,128]{2,1,0:T(8,128)S(1)}, f32[2,16,128]{2,1,0:T(8,128)S(1)}, f32[2,16,128]{2,1,0:T(8,128)S(1)}) custom-call(s32[1]{0:T(128)} %get-tuple-element.104.place, s32[40,16]{1,0:T(8,128)S(1)} %get-tuple-element.105.plan.starts.uses, ...), custom_call_target="tpu_custom_call" | custom-call | flops 75497472 | bytes 1179648 | tf_op jit(solution)/shard_map/cond/branch_1_fun/totals/pallas_call | solution.py:538
  34.6 7.5 %collective-permute-start.21 = (f32[2,16,128]{2,1,0:T(8,128)S(1)}, f32[2,16,128]{2,1,0:T(8,128)S(1)}, u32[]{:S(2)}, u32[]{:S(2)}) collective-permute-start(f32[2,16,128]{2,1,0:T(8,128)S(1)} %get-tuple-element.119), channel_id=1, source_target_pairs={{0,4},{4,8},{8,12},{12,0},{1,5},{5,9},{9,13},{13,1},{2,6},{6,10},{... | collective-permute-start | bytes 49160 | tf_op jit(solution)/shard_map/cond/branch_1_fun/ppermute | solution.py:30
  42.1 2.1 %collective-permute-start.22 = (f32[2,16,128]{2,1,0:T(8,128)S(1)}, f32[2,16,128]{2,1,0:T(8,128)S(1)}, u32[]{:S(2)}, u32[]{:S(2)}) collective-permute-start(f32[2,16,128]{2,1,0:T(8,128)S(1)} %get-tuple-element.120), channel_id=1, source_target_pairs={{0,8},{4,12},{8,0},{12,4},{1,9},{5,13},{9,1},{13,5},{2,10},{6,14},... | collective-permute-start | bytes 49160 | tf_op jit(solution)/shard_map/cond/branch_1_fun/ppermute | solution.py:30
  44.2 0.0 collective-permute-done.15.refs_4_
  44.2 0.3 collective-permute-start.23
  44.5 0.0 collective-permute-done.16.refs_5_
  44.6 0.9 %collective-permute-done.21.refs_1_ = f32[2,16,128]{2,1,0:T(8,128)S(1)} collective-permute-done((f32[2,16,128]{2,1,0:T(8,128)S(1)}, f32[2,16,128]{2,1,0:T(8,128)S(1)}, u32[]{:S(2)}, u32[]{:S(2)}) %collective-permute-start.21) | collective-permute-done | bytes 16416 | tf_op jit(solution)/shard_map/cond/branch_1_fun/ppermute | solution.py:30
  45.5 1.2 %collective-permute-done.22.refs_2_ = f32[2,16,128]{2,1,0:T(8,128)S(1)} collective-permute-done((f32[2,16,128]{2,1,0:T(8,128)S(1)}, f32[2,16,128]{2,1,0:T(8,128)S(1)}, u32[]{:S(2)}, u32[]{:S(2)}) %collective-permute-start.22) | collective-permute-done | bytes 16416 | tf_op jit(solution)/shard_map/cond/branch_1_fun/ppermute | solution.py:30
  46.7 1.2 %collective-permute-done.23.refs_3_ = f32[2,16,128]{2,1,0:T(8,128)S(1)} collective-permute-done((f32[2,16,128]{2,1,0:T(8,128)S(1)}, f32[2,16,128]{2,1,0:T(8,128)S(1)}, u32[]{:S(2)}, u32[]{:S(2)}) %collective-permute-start.23) | collective-permute-done | bytes 16416 | tf_op jit(solution)/shard_map/cond/branch_1_fun/ppermute | solution.py:30
  48.0 1.4 %items.6 = (bf16[9,2,128,128]{3,2,1,0:T(8,128)(2,1)S(1)}, bf16[3,128,128]{2,1,0:T(8,128)(2,1)S(1)}, bf16[3,128,128]{2,1,0:T(8,128)(2,1)S(1)}, bf16[3,128,128]{2,1,0:T(8,128)(2,1)S(1)}) custom-call(s32[1]{0:T(128)} %get-tuple-element.104.place, s32[40,16]{1,0:T(8,128)S(1)} %get-tuple-element.105.plan.starts.uses, bf16[1,128,2048]{2,1,0:T(8,128)(2,1)S(1)} %copy-done.2, ...), custom_call_target="tpu_custom_call" | custom-call | flops 188743680 | bytes 1179648 | tf_op jit(solution)/shard_map/cond/branch_1_fun/items/pallas_call | solution.py:614
  49.4 2.1 %collective-permute-start.27 = (bf16[3,128,128]{2,1,0:T(8,128)(2,1)S(1)}, bf16[3,128,128]{2,1,0:T(8,128)(2,1)S(1)}, u32[]{:S(2)}, u32[]{:S(2)}) collective-permute-start(bf16[3,128,128]{2,1,0:T(8,128)(2,1)S(1)} %get-tuple-element.129), channel_id=1, source_target_pairs={{0,12},{4,0},{8,4},{12,8},{1,13},{5,1},{9,5},{13,9},{2,14},{6,2},{... | collective-permute-start | bytes 294920 | tf_op jit(solution)/shard_map/cond/branch_1_fun/ppermute | solution.py:30
  51.6 0.0 collective-permute-start.28
  51.6 0.8 %collective-permute-start.29 = (bf16[3,128,128]{2,1,0:T(8,128)(2,1)S(1)}, bf16[3,128,128]{2,1,0:T(8,128)(2,1)S(1)}, u32[]{:S(2)}, u32[]{:S(2)}) collective-permute-start(bf16[3,128,128]{2,1,0:T(8,128)(2,1)S(1)} %get-tuple-element.131), channel_id=1, source_target_pairs={{0,4},{4,8},{8,12},{12,0},{1,5},{5,9},{9,13},{13,1},{2,6},{6,10},{... | collective-permute-start | bytes 294920 | tf_op jit(solution)/shard_map/cond/branch_1_fun/ppermute | solution.py:30
  52.4 2.8 %heads.7 = (bf16[3,128,128]{2,1,0:T(8,128)(2,1)S(1)}, bf16[3,128,128]{2,1,0:T(8,128)(2,1)S(1)}, bf16[3,128,128]{2,1,0:T(8,128)(2,1)S(1)}, bf16[3,128,128]{2,1,0:T(8,128)(2,1)S(1)}) custom-call(s32[3]{0:T(128)S(1)} %slice_bitcast_fusion.1.spot, s32[40,16]{1,0:T(8,128)S(1)} %get-tuple-element.105.plan.starts.uses, bf16[1,128,2048]{2,1,0:T(8,128)(2,1)S(1)} %copy-done.7, ...), custom_call_target="tpu_custom_call" | custom-call | flops 335544320 | bytes 917504 | tf_op jit(solution)/shard_map/cond/branch_1_fun/heads/pallas_call | solution.py:286
  55.3 3.1 %collective-permute-start.24 = (bf16[3,128,128]{2,1,0:T(8,128)(2,1)S(1)}, bf16[3,128,128]{2,1,0:T(8,128)(2,1)S(1)}, u32[]{:S(2)}, u32[]{:S(2)}) collective-permute-start(bf16[3,128,128]{2,1,0:T(8,128)(2,1)S(1)} %get-tuple-element.124), channel_id=1, source_target_pairs={{0,12},{4,0},{8,4},{12,8},{1,13},{5,1},{9,5},{13,9},{2,14},{6,2},{... | collective-permute-start | bytes 294920 | tf_op jit(solution)/shard_map/cond/branch_1_fun/ppermute | solution.py:30
  58.3 1.1 %collective-permute-start.25 = (bf16[3,128,128]{2,1,0:T(8,128)(2,1)S(1)}, bf16[3,128,128]{2,1,0:T(8,128)(2,1)S(1)}, u32[]{:S(2)}, u32[]{:S(2)}) collective-permute-start(bf16[3,128,128]{2,1,0:T(8,128)(2,1)S(1)} %get-tuple-element.125), channel_id=1, source_target_pairs={{0,8},{4,12},{8,0},{12,4},{1,9},{5,13},{9,1},{13,5},{2,10},{6,14},... | collective-permute-start | bytes 294920 | tf_op jit(solution)/shard_map/cond/branch_1_fun/ppermute | solution.py:30
  59.4 0.0 collective-permute-done.27.refs_0_
  59.4 0.0 collective-permute-start.26
  59.4 3.6 %own.6 = (f32[16,128,128]{2,1,0:T(8,128)S(1)}, bf16[1,128,2048]{2,1,0:T(8,128)(2,1)}, bf16[1,128,2048]{2,1,0:T(8,128)(2,1)}) custom-call(s32[1]{0:T(128)} %get-tuple-element.104.place, s32[40,16]{1,0:T(8,128)S(1)} %get-tuple-element.105.plan.starts.uses, bf16[1,128,2048]{2,1,0:T(8,128)(2,1)S(1)} %copy-done.7, bf16[1,128,2048]{2,1,0:T(8,128)(2,1)S(1)} %copy-done.2, ...), custom_call_target="tpu_custom_call" | custom-call | flops 524288000 | bytes 3276800 | tf_op jit(solution)/shard_map/cond/branch_1_fun/own/pallas_call | solution.py:671
  63.0 0.0 collective-permute-done.28.refs_1_
  63.0 0.0 collective-permute-done.29.refs_2_
  63.0 2.0 %query_gradient.6.refs_4_ = bf16[1,128,2048]{2,1,0:T(8,128)(2,1)} custom-call(s32[1]{0:T(128)} %get-tuple-element.104.place, s32[40,16]{1,0:T(8,128)S(1)} %get-tuple-element.105.plan.starts.uses, f32[16,128,128]{2,1,0:T(8,128)S(1)} %get-tuple-element.128.own_query, bf16[3,128,128]{2,1,0:T(8,128)(2,1)S(1)} %collective-permute-done.27.refs_0_, ...), custom_call_target="tpu_custom_call" | custom-call | tf_op jit(solution)/shard_map/cond/branch_1_fun/query_gradient/pallas_call | solution.py:718
  65.1 0.0 collective-permute-done.24.refs_1_
  65.1 2.0 %collective-permute-done.25.refs_2_ = bf16[3,128,128]{2,1,0:T(8,128)(2,1)S(1)} collective-permute-done((bf16[3,128,128]{2,1,0:T(8,128)(2,1)S(1)}, bf16[3,128,128]{2,1,0:T(8,128)(2,1)S(1)}, u32[]{:S(2)}, u32[]{:S(2)}) %collective-permute-start.25) | collective-permute-done | bytes 98336 | tf_op jit(solution)/shard_map/cond/branch_1_fun/ppermute | solution.py:30
  67.1 1.7 %put_shared.6 = (bf16[1,128,2048]{2,1,0:T(8,128)(2,1)}, bf16[1,128,2048]{2,1,0:T(8,128)(2,1)}, bf16[1,128,2048]{2,1,0:T(8,128)(2,1)}) custom-call(s32[1]{0:T(128)} %get-tuple-element.104.place, s32[40,16]{1,0:T(8,128)S(1)} %get-tuple-element.105.plan.starts.uses, ...), custom_call_target="tpu_custom_call", output_to_operand_aliasing={{0}: (6, {}), {1}: (7, {}), {2}: (8, {})} | custom-call | tf_op jit(solution)/shard_map/cond/branch_1_fun/put_shared/pallas_call | solution.py:754
  (9 shorter events, 0.0 us)
Async XLA Ops:
  1.4 7.0 %collective-permute-start.81 = (s32[4,4,6]{2,1,0:T(4,128)S(1)}, s32[4,4,6]{2,1,0:T(4,128)S(1)}, u32[]{:S(2)}, u32[]{:S(2)}) collective-permute-start(s32[4,4,6]{2,1,0:T(4,128)S(1)} %fusion.refs_0_), channel_id=1, source_target_pairs={{0,4},{4,8},{8,12},{12,0},{1,5},{5,9},{9,13},{13,1},{2,6},{6,10},{... | collective-permute-start | bytes 1160 | tf_op jit(solution)/shard_map/ppermute | solution.py:30
  4.4 4.6 %collective-permute-start.82 = (s32[4,4,6]{2,1,0:T(4,128)S(1)}, s32[4,4,6]{2,1,0:T(4,128)S(1)}, u32[]{:S(2)}, u32[]{:S(2)}) collective-permute-start(s32[4,4,6]{2,1,0:T(4,128)S(1)} %fusion.refs_0_), channel_id=1, source_target_pairs={{0,8},{4,12},{8,0},{12,4},{1,9},{5,13},{9,1},{13,5},{2,10},{6,14},... | collective-permute-start | bytes 1160 | tf_op jit(solution)/shard_map/ppermute | solution.py:30
  7.0 3.7 %collective-permute-start.83 = (s32[4,4,6]{2,1,0:T(4,128)S(1)}, s32[4,4,6]{2,1,0:T(4,128)S(1)}, u32[]{:S(2)}, u32[]{:S(2)}) collective-permute-start(s32[4,4,6]{2,1,0:T(4,128)S(1)} %fusion.refs_0_), channel_id=1, source_target_pairs={{0,12},{4,0},{8,4},{12,8},{1,13},{5,1},{9,5},{13,9},{2,14},{6,2},{... | collective-permute-start | bytes 1160 | tf_op jit(solution)/shard_map/ppermute | solution.py:30
  12.8 12.8 %copy-start.2 = (bf16[1,128,2048]{2,1,0:T(8,128)(2,1)S(1)}, bf16[1,128,2048]{2,1,0:T(8,128)(2,1)}, u32[]{:S(2)}) copy-start(bf16[1,128,2048]{2,1,0:T(8,128)(2,1)} %get-tuple-element.107.refs_1_.key) | copy-start | bytes 1572868 | tf_op jit(solution)/shard_map/cond
  12.8 12.8 %copy-start.7 = (bf16[1,128,2048]{2,1,0:T(8,128)(2,1)S(1)}, bf16[1,128,2048]{2,1,0:T(8,128)(2,1)}, u32[]{:S(2)}) copy-start(bf16[1,128,2048]{2,1,0:T(8,128)(2,1)} %get-tuple-element.106.query.refs_0_) | copy-start | bytes 1572868 | tf_op jit(solution)/shard_map/cond
  12.8 12.8 %copy-start.12 = (bf16[1,128,2048]{2,1,0:T(8,128)(2,1)S(1)}, bf16[1,128,2048]{2,1,0:T(8,128)(2,1)}, u32[]{:S(2)}) copy-start(bf16[1,128,2048]{2,1,0:T(8,128)(2,1)} %get-tuple-element.109.grad.refs_3_) | copy-start | bytes 1572868 | tf_op jit(solution)/shard_map/cond
  12.8 12.8 %copy-start.17 = (bf16[1,128,2048]{2,1,0:T(8,128)(2,1)S(1)}, bf16[1,128,2048]{2,1,0:T(8,128)(2,1)}, u32[]{:S(2)}) copy-start(bf16[1,128,2048]{2,1,0:T(8,128)(2,1)} %get-tuple-element.108.refs_2_.value) | copy-start | bytes 1572868 | tf_op jit(solution)/shard_map/cond
  14.4 9.7 %collective-permute-start.18 = (bf16[3,2,128,128]{3,2,1,0:T(8,128)(2,1)S(1)}, bf16[3,2,128,128]{3,2,1,0:T(8,128)(2,1)S(1)}, u32[]{:S(2)}, u32[]{:S(2)}) collective-permute-start(bf16[3,2,128,128]{3,2,1,0:T(8,128)(2,1)S(1)} %get-tuple-element.110.refs_4_), channel_id=1, source_target_pairs={{0,4},{4,8},{8,12},{12,0},{1,5},{5,9},{9,13},{13,1},{2,6},{6,10},{... | collective-permute-start | bytes 589832 | tf_op jit(solution)/shard_map/cond/branch_1_fun/ppermute | solution.py:30
  14.5 18.7 %collective-permute-start.19 = (bf16[3,2,128,128]{3,2,1,0:T(8,128)(2,1)S(1)}, bf16[3,2,128,128]{3,2,1,0:T(8,128)(2,1)S(1)}, u32[]{:S(2)}, u32[]{:S(2)}) collective-permute-start(bf16[3,2,128,128]{3,2,1,0:T(8,128)(2,1)S(1)} %get-tuple-element.111.refs_5_), channel_id=1, source_target_pairs={{0,8},{4,12},{8,0},{12,4},{1,9},{5,13},{9,1},{13,5},{2,10},{6,14},... | collective-permute-start | bytes 589832 | tf_op jit(solution)/shard_map/cond/branch_1_fun/ppermute | solution.py:30
  18.1 15.1 %collective-permute-start.20 = (bf16[3,2,128,128]{3,2,1,0:T(8,128)(2,1)S(1)}, bf16[3,2,128,128]{3,2,1,0:T(8,128)(2,1)S(1)}, u32[]{:S(2)}, u32[]{:S(2)}) collective-permute-start(bf16[3,2,128,128]{3,2,1,0:T(8,128)(2,1)S(1)} %get-tuple-element.112.refs_6_), channel_id=1, source_target_pairs={{0,12},{4,0},{8,4},{12,8},{1,13},{5,1},{9,5},{13,9},{2,14},{6,2},{... | collective-permute-start | bytes 589832 | tf_op jit(solution)/shard_map/cond/branch_1_fun/ppermute | solution.py:30
  20.6 23.7 %collective-permute-start.15 = (bf16[4,128,128]{2,1,0:T(8,128)(2,1)S(1)}, bf16[4,128,128]{2,1,0:T(8,128)(2,1)S(1)}, u32[]{:S(2)}, u32[]{:S(2)}) collective-permute-start(bf16[4,128,128]{2,1,0:T(8,128)(2,1)S(1)} %get-tuple-element.113), channel_id=1, source_target_pairs={{0,4},{4,8},{8,12},{12,0},{1,5},{5,9},{9,13},{13,1},{2,6},{6,10},{... | collective-permute-start | bytes 393224 | tf_op jit(solution)/shard_map/cond/branch_1_fun/ppermute | solution.py:30
  22.5 22.0 %collective-permute-start.16 = (bf16[4,128,128]{2,1,0:T(8,128)(2,1)S(1)}, bf16[4,128,128]{2,1,0:T(8,128)(2,1)S(1)}, u32[]{:S(2)}, u32[]{:S(2)}) collective-permute-start(bf16[4,128,128]{2,1,0:T(8,128)(2,1)S(1)} %get-tuple-element.114), channel_id=1, source_target_pairs={{0,8},{4,12},{8,0},{12,4},{1,9},{5,13},{9,1},{13,5},{2,10},{6,14},... | collective-permute-start | bytes 393224 | tf_op jit(solution)/shard_map/cond/branch_1_fun/ppermute | solution.py:30
  24.1 20.5 %collective-permute-start.17 = (bf16[4,128,128]{2,1,0:T(8,128)(2,1)S(1)}, bf16[4,128,128]{2,1,0:T(8,128)(2,1)S(1)}, u32[]{:S(2)}, u32[]{:S(2)}) collective-permute-start(bf16[4,128,128]{2,1,0:T(8,128)(2,1)S(1)} %get-tuple-element.115), channel_id=1, source_target_pairs={{0,12},{4,0},{8,4},{12,8},{1,13},{5,1},{9,5},{13,9},{2,14},{6,2},{... | collective-permute-start | bytes 393224 | tf_op jit(solution)/shard_map/cond/branch_1_fun/ppermute | solution.py:30
  34.6 10.9 %collective-permute-start.21 = (f32[2,16,128]{2,1,0:T(8,128)S(1)}, f32[2,16,128]{2,1,0:T(8,128)S(1)}, u32[]{:S(2)}, u32[]{:S(2)}) collective-permute-start(f32[2,16,128]{2,1,0:T(8,128)S(1)} %get-tuple-element.119), channel_id=1, source_target_pairs={{0,4},{4,8},{8,12},{12,0},{1,5},{5,9},{9,13},{13,1},{2,6},{6,10},{... | collective-permute-start | bytes 49160 | tf_op jit(solution)/shard_map/cond/branch_1_fun/ppermute | solution.py:30
  42.1 4.6 %collective-permute-start.22 = (f32[2,16,128]{2,1,0:T(8,128)S(1)}, f32[2,16,128]{2,1,0:T(8,128)S(1)}, u32[]{:S(2)}, u32[]{:S(2)}) collective-permute-start(f32[2,16,128]{2,1,0:T(8,128)S(1)} %get-tuple-element.120), channel_id=1, source_target_pairs={{0,8},{4,12},{8,0},{12,4},{1,9},{5,13},{9,1},{13,5},{2,10},{6,14},... | collective-permute-start | bytes 49160 | tf_op jit(solution)/shard_map/cond/branch_1_fun/ppermute | solution.py:30
  44.2 3.7 %collective-permute-start.23 = (f32[2,16,128]{2,1,0:T(8,128)S(1)}, f32[2,16,128]{2,1,0:T(8,128)S(1)}, u32[]{:S(2)}, u32[]{:S(2)}) collective-permute-start(f32[2,16,128]{2,1,0:T(8,128)S(1)} %get-tuple-element.121), channel_id=1, source_target_pairs={{0,12},{4,0},{8,4},{12,8},{1,13},{5,1},{9,5},{13,9},{2,14},{6,2},{... | collective-permute-start | bytes 49160 | tf_op jit(solution)/shard_map/cond/branch_1_fun/ppermute | solution.py:30
  49.4 10.0 %collective-permute-start.27 = (bf16[3,128,128]{2,1,0:T(8,128)(2,1)S(1)}, bf16[3,128,128]{2,1,0:T(8,128)(2,1)S(1)}, u32[]{:S(2)}, u32[]{:S(2)}) collective-permute-start(bf16[3,128,128]{2,1,0:T(8,128)(2,1)S(1)} %get-tuple-element.129), channel_id=1, source_target_pairs={{0,12},{4,0},{8,4},{12,8},{1,13},{5,1},{9,5},{13,9},{2,14},{6,2},{... | collective-permute-start | bytes 294920 | tf_op jit(solution)/shard_map/cond/branch_1_fun/ppermute | solution.py:30
  51.6 11.5 %collective-permute-start.28 = (bf16[3,128,128]{2,1,0:T(8,128)(2,1)S(1)}, bf16[3,128,128]{2,1,0:T(8,128)(2,1)S(1)}, u32[]{:S(2)}, u32[]{:S(2)}) collective-permute-start(bf16[3,128,128]{2,1,0:T(8,128)(2,1)S(1)} %get-tuple-element.130), channel_id=1, source_target_pairs={{0,8},{4,12},{8,0},{12,4},{1,9},{5,13},{9,1},{13,5},{2,10},{6,14},... | collective-permute-start | bytes 294920 | tf_op jit(solution)/shard_map/cond/branch_1_fun/ppermute | solution.py:30
  51.6 11.5 %collective-permute-start.29 = (bf16[3,128,128]{2,1,0:T(8,128)(2,1)S(1)}, bf16[3,128,128]{2,1,0:T(8,128)(2,1)S(1)}, u32[]{:S(2)}, u32[]{:S(2)}) collective-permute-start(bf16[3,128,128]{2,1,0:T(8,128)(2,1)S(1)} %get-tuple-element.131), channel_id=1, source_target_pairs={{0,4},{4,8},{8,12},{12,0},{1,5},{5,9},{9,13},{13,1},{2,6},{6,10},{... | collective-permute-start | bytes 294920 | tf_op jit(solution)/shard_map/cond/branch_1_fun/ppermute | solution.py:30
  55.3 9.8 %collective-permute-start.24 = (bf16[3,128,128]{2,1,0:T(8,128)(2,1)S(1)}, bf16[3,128,128]{2,1,0:T(8,128)(2,1)S(1)}, u32[]{:S(2)}, u32[]{:S(2)}) collective-permute-start(bf16[3,128,128]{2,1,0:T(8,128)(2,1)S(1)} %get-tuple-element.124), channel_id=1, source_target_pairs={{0,12},{4,0},{8,4},{12,8},{1,13},{5,1},{9,5},{13,9},{2,14},{6,2},{... | collective-permute-start | bytes 294920 | tf_op jit(solution)/shard_map/cond/branch_1_fun/ppermute | solution.py:30
  58.3 8.8 %collective-permute-start.25 = (bf16[3,128,128]{2,1,0:T(8,128)(2,1)S(1)}, bf16[3,128,128]{2,1,0:T(8,128)(2,1)S(1)}, u32[]{:S(2)}, u32[]{:S(2)}) collective-permute-start(bf16[3,128,128]{2,1,0:T(8,128)(2,1)S(1)} %get-tuple-element.125), channel_id=1, source_target_pairs={{0,8},{4,12},{8,0},{12,4},{1,9},{5,13},{9,1},{13,5},{2,10},{6,14},... | collective-permute-start | bytes 294920 | tf_op jit(solution)/shard_map/cond/branch_1_fun/ppermute | solution.py:30
  59.4 7.7 %collective-permute-start.26 = (bf16[3,128,128]{2,1,0:T(8,128)(2,1)S(1)}, bf16[3,128,128]{2,1,0:T(8,128)(2,1)S(1)}, u32[]{:S(2)}, u32[]{:S(2)}) collective-permute-start(bf16[3,128,128]{2,1,0:T(8,128)(2,1)S(1)} %get-tuple-element.126), channel_id=1, source_target_pairs={{0,4},{4,8},{8,12},{12,0},{1,5},{5,9},{9,13},{13,1},{2,6},{6,10},{... | collective-permute-start | bytes 294920 | tf_op jit(solution)/shard_map/cond/branch_1_fun/ppermute | solution.py:30
